TPU v7x, 256 devices: a whole 4x4x8 slice. The times are simulated.
256 devices in a mesh: rx: 8 (over y_lo, x), ry: 8 (over z), tp: 4 (over y_hi, core).
Axes of the slice: x: 4, y: 4 (y_hi: 2, y_lo: 2; y = y_hi * 2 + y_lo), z: 8, core: 2. Of those that a mesh axis runs over, the one named last changes fastest.
Arguments:
- inputs: bfloat16 [8, 8, 512, 6144], P('rx', 'ry', None, 'tp'), may hold values from -6 to 6
- out_grads: bfloat16 [8, 8, 512, 6144], P('rx', 'ry', None, 'tp'), may hold values from -6 to 6
- up_weight: bfloat16 [8, 8, 256, 6144], P('rx', 'ry', 'tp'), may hold values from -6 to 6
- down_weight: bfloat16 [8, 8, 256, 6144], P('rx', 'ry', 'tp'), may hold values from -6 to 6
- group_x: int32 [8, 8], replicated, may hold values from 0 to 1
- group_y: int32 [8, 8], replicated, may hold values from 0 to 1
Outputs:
- input_grads: bfloat16 [8, 8, 512, 6144], P('rx', 'ry', None, 'tp')
- new_up: bfloat16 [8, 8, 256, 6144], P('rx', 'ry', 'tp')
- new_down: bfloat16 [8, 8, 256, 6144], P('rx', 'ry', 'tp')
Inputs may be any that keep to these rules, and one draw needn't show every extreme that they name: `group_x`: group labels; replicas of one line with equal labels form one group. `group_y`: group labels; replicas of one line with equal labels form one group.
All inputs are finite; a program needn't handle non-finite values.
Results may differ from a plain program's by a relative error of at most 0.02.
Values may be sent and summed in bfloat16 or wider, within the bound.
No kernel may reach another device: no remote copies, remote signals or barrier semaphores. Data moves between devices by JAX's collectives and lax.ppermute only.
A program may use at most 128 MiB of HBM per device.

v0:
```python
import jax
import jax.numpy as jnp
from jax import lax
from jax.sharding import PartitionSpec as P

D = 6144
GROUPS = 2


learn_rate = 0.5
inv_root_two = 0.7071067811865476
inv_root_tau = 0.3989422804014327


def mult_rows(left, right):
    return lax.dot_general(
        left, right, (((1,), (1,)), ((), ())), preferred_element_type=jnp.float32
    )


def mult_cols(left, right):
    return lax.dot_general(
        left, right, (((0,), (0,)), ((), ())), preferred_element_type=jnp.float32
    )


def local_grads(pre, hid_grad):
    cdf = 0.5 * (1.0 + jax.scipy.special.erf(pre * inv_root_two))
    act = (pre * cdf).astype(jnp.bfloat16)
    pre_grad = (hid_grad * (cdf + pre * jnp.exp(-0.5 * pre * pre) * inv_root_tau)).astype(
        jnp.bfloat16
    )
    return (act, pre_grad)


def stacked(weights, slot_mask):
    return jnp.where(slot_mask[:, None, None], weights.astype(jnp.float32)[None], 0.0)


def picked(sums, slot_mask, members):
    chosen = jnp.sum(sums * slot_mask[:, None, None].astype(jnp.float32), axis=0)
    return (chosen / members).astype(jnp.bfloat16)


def shards(inputs, out_grads, up_weight, down_weight, group_x, group_y):
    x_local = inputs[0, 0]
    dy_local = out_grads[0, 0]
    up_local = up_weight[0, 0]
    down_local = down_weight[0, 0]
    scale_in = D ** (-0.5)
    scale_hid = (up_local.shape[0] * lax.axis_size("tp")) ** (-0.5)
    x_whole = lax.all_gather(x_local, "tp", axis=1, tiled=True)
    dy_whole = lax.all_gather(dy_local, "tp", axis=1, tiled=True)
    pre = mult_rows(x_whole, up_local) * scale_in
    hid_grad = mult_rows(dy_whole, down_local) * scale_hid
    act, pre_grad = local_grads(pre, hid_grad)
    partial_grad = jnp.dot(pre_grad, up_local, preferred_element_type=jnp.float32) * scale_in
    grad_up = mult_cols(pre_grad, x_whole) * scale_in
    grad_down = mult_cols(act, dy_whole) * scale_hid
    in_grad = lax.psum_scatter(
        partial_grad.astype(jnp.bfloat16), "tp", scatter_dimension=1, tiled=True
    )
    own_up, own_down = (up_local, down_local)
    step_up = (own_up.astype(jnp.float32) - learn_rate * grad_up).astype(jnp.bfloat16)
    step_down = (own_down.astype(jnp.float32) - learn_rate * grad_down).astype(jnp.bfloat16)
    first_pos = lax.axis_index("rx")
    second_pos = lax.axis_index("ry")
    slots = jnp.arange(GROUPS, dtype=jnp.int32)
    line_first = group_x[second_pos]
    label_first = line_first[first_pos]
    members_first = jnp.sum((line_first == label_first).astype(jnp.float32))
    mask_first = slots == label_first
    sums_up, sums_down = (
        lax.psum(stacked(step_up, mask_first).astype(jnp.bfloat16), "rx").astype(jnp.float32),
        lax.psum(stacked(step_down, mask_first).astype(jnp.bfloat16), "rx").astype(jnp.float32),
    )
    mid_up = picked(sums_up, mask_first, members_first)
    mid_down = picked(sums_down, mask_first, members_first)
    line_second = group_y[first_pos]
    label_second = line_second[second_pos]
    members_second = jnp.sum((line_second == label_second).astype(jnp.float32))
    mask_second = slots == label_second
    sums_up, sums_down = (
        lax.psum(stacked(mid_up, mask_second).astype(jnp.bfloat16), "ry").astype(jnp.float32),
        lax.psum(stacked(mid_down, mask_second).astype(jnp.bfloat16), "ry").astype(jnp.float32),
    )
    final_up = picked(sums_up, mask_second, members_second)
    final_down = picked(sums_down, mask_second, members_second)
    return (in_grad[None, None], final_up[None, None], final_down[None, None])


def solution(mesh):
    in_specs = (
        P("rx", "ry", None, "tp"),
        P("rx", "ry", None, "tp"),
        P("rx", "ry", "tp", None),
        P("rx", "ry", "tp", None),
        P(),
        P(),
    )
    out_specs = (P("rx", "ry", None, "tp"), P("rx", "ry", "tp", None), P("rx", "ry", "tp", None))
    return jax.shard_map(shards, mesh=mesh, in_specs=in_specs, out_specs=out_specs, check_vma=False)
```

profile of v0, /device:TPU:24, one launch (start us, length us, event | category | flops | bytes accessed | tf_op | source)
XLA Modules:
  0.0 403.5 jit_solution(9124705707752181604)
XLA Ops:
  7.2 0.7 all-gather.7.cloned.1.call-update
  8.0 0.7 all-gather.5.cloned.1.call-update
  8.7 1.3 dynamic_slice.13
  10.0 0.6 iota_compare_fusion
  10.7 53.3 %all-gather.7.cloned.1.call-done = bf16[1,1,512,6144]{3,2,1,0:T(8,128)(2,1)} async-done(((bf16[1,1,512,1536]{3,2,1,0:T(8,128)(2,1)}), bf16[1,1,512,6144]{3,2,1,0:T(8,128)(2,1)}) %all-gather.7.cloned.1.call-update) | async-done | bytes 6291472 | tf_op jit(solution)/shard_map/all_gather | solution.py:52
  64.0 4.8 %fusion.7 = f32[512,64]{0,1:T(8,128)S(1)} fusion(bf16[1,1,512,6144]{3,2,1,0:T(8,128)(2,1)} %all-gather.7.cloned.1.call-done, bf16[1,1,64,6144]{3,2,1,0:T(8,128)(2,1)S(1)} %copy-done), kind=kOutput, calls=%fused_computation.10 | convolution fusion | flops 402653184 | bytes 7208960 | tf_op jit(solution)/shard_map/dot_general | solution.py:16
  68.8 49.5 %all-gather.5.cloned.1.call-done = bf16[1,1,512,6144]{3,2,1,0:T(8,128)(2,1)} async-done(((bf16[1,1,512,1536]{3,2,1,0:T(8,128)(2,1)}), bf16[1,1,512,6144]{3,2,1,0:T(8,128)(2,1)}) %all-gather.5.cloned.1.call-update) | async-done | bytes 6291472 | tf_op jit(solution)/shard_map/all_gather | solution.py:53
  118.2 5.0 %fusion.18 = bf16[512,64]{0,1:T(8,128)(2,1)S(1)} fusion(bf16[1,1,512,6144]{3,2,1,0:T(8,128)(2,1)} %all-gather.5.cloned.1.call-done, bf16[1,1,64,6144]{3,2,1,0:T(8,128)(2,1)S(1)} %copy-done.1, f32[512,64]{0,1:T(8,128)S(1)} %fusion.7), kind=kOutput, calls=%fused_computation.29 | convolution fusion | flops 403046400 | bytes 7274496 | tf_op jit(solution)/shard_map/dot_general | solution.py:16
  123.2 4.1 %fusion.3 = bf16[64,6144]{1,0:T(8,128)(2,1)S(1)} fusion(bf16[1,1,512,6144]{3,2,1,0:T(8,128)(2,1)} %all-gather.5.cloned.1.call-done, bf16[1,1,64,6144]{3,2,1,0:T(8,128)(2,1)S(1)} %copy-done.1, f32[512,64]{0,1:T(8,128)S(1)} %fusion.7), kind=kOutput, calls=%fused_computation.6 | convolution fusion | flops 404422656 | bytes 7995392 | tf_op jit(solution)/shard_map/dot_general | solution.py:22
  127.4 1.2 fusion.5
  128.6 2.3 select_convert_fusion.3
  131.0 1.3 dynamic_slice.12
  132.3 1.9 fusion.29
  135.5 91.8 %all-reduce.7.cloned.1.call-done = (bf16[2,64,6144]{2,1,0:T(8,128)(2,1)}, bf16[2,64,6144]{2,1,0:T(8,128)(2,1)}) async-done(((bf16[2,64,6144]{2,1,0:T(8,128)(2,1)}, bf16[2,64,6144]{2,1,0:T(8,128)(2,1)}), (bf16[2,64,6144]{2,1,0:T(8,128)(2,1)}, bf16[2,64,6144]{2,1,0:T(8,128)(2,1)})) %all-reduce.7.cloned.1.call-update) | async-done | bytes 3145744 | tf_op jit(solution)/shard_map/psum | solution.py:75
  227.3 3.1 multiply_reduce_fusion.1
  230.4 0.9 fusion.21
  231.3 2.3 select_convert_fusion.2
  233.7 4.5 %multiply_convert_fusion = bf16[512,6144]{1,0:T(8,128)(2,1)} fusion(bf16[512,64]{0,1:T(8,128)(2,1)S(1)} %fusion.18, bf16[1,1,64,6144]{3,2,1,0:T(8,128)(2,1)S(1)} %copy-done), kind=kOutput, calls=%fused_computation | convolution fusion | flops 408944640 | bytes 7143424 | tf_op jit(solution)/shard_map/dot_general | solution.py:57
  238.1 1.9 fusion.30
  240.7 85.4 %all-reduce.5.cloned.1.call-done = (bf16[2,64,6144]{2,1,0:T(8,128)(2,1)}, bf16[2,64,6144]{2,1,0:T(8,128)(2,1)}) async-done(((bf16[2,64,6144]{2,1,0:T(8,128)(2,1)}, bf16[2,64,6144]{2,1,0:T(8,128)(2,1)}), (bf16[2,64,6144]{2,1,0:T(8,128)(2,1)}, bf16[2,64,6144]{2,1,0:T(8,128)(2,1)})) %all-reduce.5.cloned.1.call-update) | async-done | bytes 3145744 | tf_op jit(solution)/shard_map/psum | solution.py:85
  326.2 3.1 multiply_reduce_fusion
  329.2 1.6 fusion.27
  330.8 1.6 fusion.26
  332.4 64.5 %reduce-scatter.2.cloned.1.call-done = bf16[512,1536]{1,0:T(8,128)(2,1)} async-done(((bf16[512,6144]{1,0:T(8,128)(2,1)}), bf16[512,1536]{1,0:T(8,128)(2,1)}) %reduce-scatter.2.cloned.1.call-update) | async-done | bytes 1572880 | tf_op jit(solution)/shard_map/reduce_scatter | solution.py:60
  (20 shorter events, 2.2 us)
Async XLA Ops:
  7.2 56.8 %copy-start = (bf16[1,1,64,6144]{3,2,1,0:T(8,128)(2,1)S(1)}, bf16[1,1,64,6144]{3,2,1,0:T(8,128)(2,1)}, u32[]{:S(2)}) copy-start(bf16[1,1,64,6144]{3,2,1,0:T(8,128)(2,1)} %param.8) | copy-start | bytes 2359300
  7.2 56.8 %all-gather.7.cloned.1.call-start = ((), (), s32[]{:S(2)}) async-start(), calls=%async_computation.3 | async-start | bytes 7864320 | tf_op jit(solution)/shard_map/all_gather | solution.py:52
  7.9 110.3 %all-gather.5.cloned.1.call-start = ((), (), s32[]{:S(2)}) async-start(), calls=%async_computation.2 | async-start | bytes 7864320 | tf_op jit(solution)/shard_map/all_gather | solution.py:53
  8.7 218.7 %all-reduce.7.cloned.1.call-start = ((), (), s32[]{:S(2)}) async-start(), calls=%async_computation.5 | async-start | bytes 6291456 | tf_op jit(solution)/shard_map/psum | solution.py:75
  10.7 107.6 %copy-start.1 = (bf16[1,1,64,6144]{3,2,1,0:T(8,128)(2,1)S(1)}, bf16[1,1,64,6144]{3,2,1,0:T(8,128)(2,1)}, u32[]{:S(2)}) copy-start(bf16[1,1,64,6144]{3,2,1,0:T(8,128)(2,1)} %param.9) | copy-start | bytes 2359300
  118.2 9.1 %slice-start = ((s8[6291456]{0:T(1024)(128)(4,1)}), s8[4194304]{0:T(1024)(128)(4,1)S(1)}, s32[]{:S(2)}) async-start(s8[6291456]{0:T(1024)(128)(4,1)} %bitcast.35), calls=%async_computation.6 | async-start | bytes 8388608
  123.2 4.2 %slice-start.1 = ((s8[6291456]{0:T(1024)(128)(4,1)}), s8[2097152]{0:T(1024)(128)(4,1)S(1)}, s32[]{:S(2)}) async-start(s8[6291456]{0:T(1024)(128)(4,1)} %bitcast.35), calls=%async_computation.7 | async-start | bytes 4194304
  130.9 195.2 %all-reduce.5.cloned.1.call-start = ((), (), s32[]{:S(2)}) async-start(), calls=%async_computation.4 | async-start | bytes 6291456 | tf_op jit(solution)/shard_map/psum | solution.py:85
  233.6 163.3 %reduce-scatter.2.cloned.1.call-start = ((), (), s32[]{:S(2)}) async-start(), calls=%async_computation.1 | async-start | bytes 7864320 | tf_op jit(solution)/shard_map/reduce_scatter | solution.py:60
Sparse Core Ops, SparseCore 0:
  9.8 54.0 all-gather.6
  65.8 52.4 all-gather.4
  131.1 96.2 all-reduce.6
  233.7 92.3 all-reduce.4
  329.4 67.5 reduce-scatter.1
where the time goes:
time: 407 us; the launch traced here: 403 us
  waiting for transfers between devices  346 us (85%)
  other arithmetic  21.2 us (5%)
  matrix products  19.6 us (5%)
  between operations  13.9 us (3%)
    psum x1, waiting for transfers between devices, shards(): lax.psum(stacked(step_down, mask_first).astype(jnp.bfloat16), 'rx')  91.8 us
    psum x1, waiting for transfers between devices, shards(): lax.psum(stacked(mid_down, mask_second).astype(jnp.bfloat16), 'ry')  85.4 us
    reduce_scatter x1, waiting for transfers between devices, shards(): lax.psum_scatter(partial_grad.astype(jnp.bfloat16), 'tp', scatter_dimensi...  64.5 us
    all_gather x1, waiting for transfers between devices, shards(): x_whole = lax.all_gather(x_local, 'tp', axis=1, tiled=True)  53.3 us
    all_gather x1, waiting for transfers between devices, shards(): dy_whole = lax.all_gather(dy_local, 'tp', axis=1, tiled=True)  49.5 us
    dot_general x2, matrix products, mult_rows(): lax.dot_general(left, right, (((1,), (1,)), ((), ())), preferred_element_...  9.77 us
  transfers between devices with their start and end apart: 5, of which 5 were waited for; matrix products, arithmetic and copies ran while one was open for 6% of the time, Pallas kernels for 0%

commit v1 on v0

v1 whole, which is shorter than its diff:
```python
import jax
import jax.numpy as jnp
from jax import lax
from jax.sharding import PartitionSpec as P

GROUPS = 2

learn_rate = 0.5
inv_root_two = 0.7071067811865476
inv_root_tau = 0.3989422804014327


def dot(left, right, dims):
    return lax.dot_general(left, right, (dims, ((), ())), preferred_element_type=jnp.float32)


def group_means(terms, labels):
    terms = terms.astype(jnp.float32)
    means = []
    for slot in range(GROUPS):
        member = (labels == slot).astype(jnp.float32)
        total = sum(terms[k] * member[k] for k in range(terms.shape[0]))
        means.append((total / jnp.maximum(jnp.sum(member), 1.0)).astype(jnp.bfloat16))
    return jnp.stack(means)


def shards(inputs, out_grads, up_weight, down_weight, group_x, group_y):
    x = inputs[0, 0]
    dy = out_grads[0, 0]
    tok, feat = x.shape
    rows, width = up_weight.shape[2:]
    n_tp = lax.axis_size("tp")
    n_rx = lax.axis_size("rx")
    n_ry = lax.axis_size("ry")
    hid = rows * n_tp
    scale_in = width ** (-0.5)
    scale_hid = hid ** (-0.5)
    first_pos = lax.axis_index("rx")
    second_pos = lax.axis_index("ry")

    both = jnp.stack([up_weight[0, 0], down_weight[0, 0]])
    both = both.reshape(2, rows, n_tp, feat).transpose(2, 0, 1, 3)
    both = lax.all_to_all(both, "tp", 0, 0)
    up = both[:, 0].reshape(hid, feat)
    down = both[:, 1].reshape(hid, feat)

    pre_part = dot(x, up, ((1,), (1,))).astype(jnp.bfloat16)
    hid_part = dot(dy, down, ((1,), (1,))).astype(jnp.bfloat16)
    parts = jnp.stack([pre_part, hid_part]).reshape(2, n_tp, tok // n_tp, hid).transpose(1, 0, 2, 3)
    parts = lax.all_to_all(parts, "tp", 0, 0)
    sums = jnp.sum(parts.astype(jnp.float32), axis=0)
    pre = sums[0] * scale_in
    hid_grad = sums[1] * scale_hid
    cdf = 0.5 * (1.0 + lax.erf(pre * inv_root_two))
    act = (pre * cdf).astype(jnp.bfloat16)
    pre_grad = (hid_grad * (cdf + pre * jnp.exp(-0.5 * pre * pre) * inv_root_tau)).astype(jnp.bfloat16)
    own = jnp.stack([act, pre_grad])
    whole = lax.all_to_all(jnp.broadcast_to(own[None], (n_tp,) + own.shape), "tp", 0, 0)
    act = whole[:, 0].reshape(tok, hid)
    pre_grad = whole[:, 1].reshape(tok, hid)

    in_grad = (dot(pre_grad, up, ((1,), (0,))) * scale_in).astype(jnp.bfloat16)
    grad_up = dot(pre_grad, x, ((0,), (0,))) * scale_in
    grad_down = dot(act, dy, ((0,), (0,))) * scale_hid
    step_up = (up.astype(jnp.float32) - learn_rate * grad_up).astype(jnp.bfloat16)
    step_down = (down.astype(jnp.float32) - learn_rate * grad_down).astype(jnp.bfloat16)

    slab = rows // n_rx
    quarter = feat // (n_ry // 2)
    steps = jnp.stack([step_up, step_down]).reshape(2, n_tp, n_rx, slab, feat)
    steps = lax.all_to_all(steps.transpose(2, 0, 1, 3, 4), "rx", 0, 0)
    mids = group_means(steps, group_x[second_pos])

    mids = mids.reshape(GROUPS, 2, n_tp, slab, n_ry // 2, quarter).transpose(1, 4, 2, 0, 3, 5)
    mids = mids.reshape(n_ry * n_tp, GROUPS, slab, quarter)
    mids = lax.all_to_all(mids, ("ry", "tp"), 0, 0)
    mids = mids.reshape(n_ry, n_tp, GROUPS, slab, quarter)
    news = []
    for i in range(n_rx):
        chosen = group_x[:, i][:, None, None, None] == 0
        news.append(group_means(jnp.where(chosen, mids[:, :, 0], mids[:, :, 1]), group_y[i]))
    news = jnp.stack(news)
    news = lax.all_to_all(news, "rx", 0, 0)
    labels = group_y[first_pos]
    news = jnp.where(labels[:, None, None, None, None] == 0, news[None, :, 0], news[None, :, 1])
    news = lax.all_to_all(news, "ry", 0, 0)
    news = news.reshape(2, n_ry // 2, n_rx, n_tp, slab, quarter).transpose(0, 2, 4, 3, 1, 5)
    news = news.reshape(2, rows, width)
    return (in_grad[None, None], news[0][None, None], news[1][None, None])


def solution(mesh):
    in_specs = (
        P("rx", "ry", None, "tp"),
        P("rx", "ry", None, "tp"),
        P("rx", "ry", "tp", None),
        P("rx", "ry", "tp", None),
        P(),
        P(),
    )
    out_specs = (P("rx", "ry", None, "tp"), P("rx", "ry", "tp", None), P("rx", "ry", "tp", None))
    return jax.shard_map(shards, mesh=mesh, in_specs=in_specs, out_specs=out_specs, check_vma=False)
```

time: 407 us -> 276 us (0.68)
  waiting for transfers between devices: 346 us -> 50.8 us
  other arithmetic: 21.2 us -> 98.4 us
  blocking collectives: 0 us -> 59.4 us
  starting transfers between devices: 0.2 us -> 21.2 us
  local copies, waits for them, and re-layouts: 2.6 us -> 22.3 us
  matrix products: 19.6 us -> 6.9 us
    psum x2 -> x0, waiting for transfers between devices: 177 us -> none  [the longest x1 91.8 us: shards(): lax.psum(stacked(step_down, mask_first).astype(jnp.bfloat16), 'rx')]
    all_gather x2 -> x0, waiting for transfers between devices: 103 us -> none  [the longest x1 53.3 us: shards(): x_whole = lax.all_gather(x_local, 'tp', axis=1, tiled=True)]
    convert_element_type x7 -> x23, other arithmetic: 9.94 us -> 93 us  [the longest x18 92.2 us: group_means(): (total / jnp.maximum(jnp.sum(member), 1.0)).astype(jnp.bfloat16)]
    reduce_scatter x1 -> x0, waiting for transfers between devices: 64.5 us -> none  [shards(): lax.psum_scatter(partial_grad.astype(jnp.bfloat16), 'tp', scatter_dimensi...]
    all_to_all x0 -> x4, blocking collectives: none -> 59.4 us  [the longest x1 23 us: shards(): both = lax.all_to_all(both, 'tp', 0, 0)]
    all_to_all x0 -> x3, waiting for transfers between devices: none -> 50.8 us  [the longest x1 35.2 us: shards(): news = lax.all_to_all(news, 'ry', 0, 0)]
    all_to_all x0 -> x3, starting transfers between devices: none -> 21.2 us  [the longest x1 11.6 us: shards(): mids = lax.all_to_all(mids, ('ry', 'tp'), 0, 0)]
    dot_general x5, matrix products: 19.6 us -> 6.9 us  [dot(): lax.dot_general(left, right, (dims, ((), ())), preferred_element_type=jnp...]
  transfers between devices with their start and end apart: 5 -> 3, of which waited for: 5 -> 3; matrix products, arithmetic and copies ran while one was open for 6% -> 4% of each run, Pallas kernels for 0% -> 0%
where the time goes in v1:
time: 276 us; the launch traced here: 271 us
  other arithmetic  98.4 us (36%)
  blocking collectives  59.4 us (22%)
  waiting for transfers between devices  50.8 us (18%)
  local copies, waits for them, and re-layouts  22.3 us (8%)
  starting transfers between devices  21.2 us (8%)
  between operations  12.2 us (4%)
  matrix products  6.9 us (2%)
    convert_element_type x18, other arithmetic, group_means(): (total / jnp.maximum(jnp.sum(member), 1.0)).astype(jnp.bfloat16)  92.2 us
    all_to_all x1, waiting for transfers between devices, shards(): news = lax.all_to_all(news, 'ry', 0, 0)  35.2 us
    all_to_all x1, blocking collectives, shards(): both = lax.all_to_all(both, 'tp', 0, 0)  23 us
    all_to_all x1, blocking collectives, shards(): lax.all_to_all(jnp.broadcast_to(own[None], (n_tp,) + own.shape), 'tp', 0, 0)  12.7 us
    all_to_all x1, blocking collectives, shards(): parts = lax.all_to_all(parts, 'tp', 0, 0)  12.7 us
    all_to_all x1, starting transfers between devices, shards(): mids = lax.all_to_all(mids, ('ry', 'tp'), 0, 0)  11.6 us
    all_to_all x1, blocking collectives, shards(): news = lax.all_to_all(news, 'rx', 0, 0)  10.9 us
    all_to_all x1, waiting for transfers between devices, shards(): mids = lax.all_to_all(mids, ('ry', 'tp'), 0, 0)  10.4 us
  transfers between devices with their start and end apart: 3, of which 3 were waited for; matrix products, arithmetic and copies ran while one was open for 4% of the time, Pallas kernels for 0%

profile of v1, /device:TPU:24, one launch (start us, length us, event | category | flops | bytes accessed | tf_op | source)
XLA Modules:
  0.0 271.2 jit_solution(2486691108232384771)
XLA Ops:
  6.8 23.0 %all_to_all.35 = bf16[4,2,64,1536]{3,2,1,0:T(8,128)(2,1)S(1)} all-to-all(bf16[4,2,64,1536]{3,2,1,0:T(8,128)(2,1)S(1)} %copy.39), channel_id=1, replica_groups=mesh['rx'=8,'ry'=8,'tp'=4] {'tp'}, dimensions={0} | all-to-all | bytes 3145728 | tf_op jit(solution)/shard_map/all_to_all | solution.py:43
  34.0 12.7 %all_to_all.36 = bf16[4,2,128,256]{2,3,1,0:T(8,128)(2,1)S(1)} all-to-all(bf16[4,2,128,256]{2,3,1,0:T(8,128)(2,1)S(1)} %maximum_bitcast_fusion.1), channel_id=1, replica_groups=mesh['rx'=8,'ry'=8,'tp'=4] {'tp'}, dimensions={0} | all-to-all | bytes 1048576 | tf_op jit(solution)/shard_map/all_to_all | solution.py:50
  47.1 12.7 %all_to_all.37 = bf16[4,2,128,256]{3,2,1,0:T(8,128)(2,1)S(1)} all-to-all(bf16[4,2,128,256]{3,2,1,0:T(8,128)(2,1)S(1)} %broadcast_in_dim.80), channel_id=1, replica_groups=mesh['rx'=8,'ry'=8,'tp'=4] {'tp'}, dimensions={0} | all-to-all | bytes 1048576 | tf_op jit(solution)/shard_map/all_to_all | solution.py:58
  63.4 5.9 %all-to-all-start.3 = ((bf16[8,2,4,8,1536]{4,3,2,1,0:T(8,128)(2,1)}), bf16[8,2,4,8,1536]{4,3,2,1,0:T(8,128)(2,1)S(1)}, u32[]{:S(2)}, u32[]{:S(2)}) async-start(bf16[8,2,4,8,1536]{4,3,2,1,0:T(8,128)(2,1)} %copy_bitcast_fusion), calls=%async_computation.3 | async-start | bytes 3145728 | tf_op jit(solution)/shard_map/all_to_all | solution.py:71
  84.1 5.2 %all-to-all-done.3 = bf16[8,2,4,8,1536]{4,3,2,1,0:T(8,128)(2,1)S(1)} async-done(((bf16[8,2,4,8,1536]{4,3,2,1,0:T(8,128)(2,1)}), bf16[8,2,4,8,1536]{4,3,2,1,0:T(8,128)(2,1)S(1)}, u32[]{:S(2)}, u32[]{:S(2)}) %all-to-all-start.3) | async-done | bytes 1572896 | tf_op jit(solution)/shard_map/all_to_all | solution.py:71
  91.3 5.2 %divide_convert_fusion.1 = bf16[1,2,4,8,1536]{4,3,2,1,0:T(8,128)(2,1)S(1)} fusion(f32[8,2,4,8,1536]{4,3,2,1,0:T(8,128)S(1)} %convert_element_type.221, f32[]{:T(128)S(6)} %max.54, f32[]{:T(128)} %bitcast.22, f32[]{:T(128)} %bitcast.21, f32[]{:T(128)} %bitcast.20, f32[]{:T(128)} %bitcast.19, f32[]{:T(128)} %bitcast.18, f32[]{:T(128)} %bitcast.17, ...), kind=kLoop, calls=%fused_computation.27 | loop fusion | flops 1671168 | bytes 3342372 | tf_op jit(solution)/shard_map/convert_element_type | solution.py:23
  96.5 7.1 %divide_convert_fusion = bf16[1,2,4,8,1536]{4,3,2,1,0:T(8,128)(2,1)S(1)} fusion(f32[8,2,4,8,1536]{4,3,2,1,0:T(8,128)} %copy-done.1, f32[]{:T(128)S(6)} %max.55, f32[]{:T(128)} %bitcast.30, f32[]{:T(128)} %bitcast.29, f32[]{:T(128)} %bitcast.28, f32[]{:T(128)} %bitcast.27, f32[]{:T(128)} %bitcast.26, f32[]{:T(128)} %bitcast.25, f32[]{:T(128)} %bitcast.24, ...), kind=kLoop, calls=%fused_computation.26 | loop fusion | flops 1671168 | bytes 3342372 | tf_op jit(solution)/shard_map/convert_element_type | solution.py:23
  104.8 11.6 %all-to-all-start.4 = ((bf16[32,2,8,384]{3,2,1,0:T(8,128)(2,1)}), bf16[32,2,8,384]{3,2,1,0:T(8,128)(2,1)S(1)}, u32[]{:S(2)}, u32[]{:S(2)}) async-start(bf16[32,2,8,384]{3,2,1,0:T(8,128)(2,1)} %bitcast.32), calls=%async_computation.4 | async-start | bytes 786432 | tf_op jit(solution)/shard_map/all_to_all | solution.py:76
  120.9 10.4 %all-to-all-done.4 = bf16[32,2,8,384]{3,2,1,0:T(8,128)(2,1)S(1)} async-done(((bf16[32,2,8,384]{3,2,1,0:T(8,128)(2,1)}), bf16[32,2,8,384]{3,2,1,0:T(8,128)(2,1)S(1)}, u32[]{:S(2)}, u32[]{:S(2)}) %all-to-all-start.4) | async-done | bytes 393248 | tf_op jit(solution)/shard_map/all_to_all | solution.py:76
  131.4 5.1 %divide_convert_fusion.17 = bf16[1,4,8,384]{3,2,1,0:T(8,128)(2,1)S(1)} fusion(f32[8,4,8,384]{3,2,1,0:T(8,128)S(1)} %get-tuple-element.46, f32[]{:T(128)S(6)} %max.56, f32[]{:T(128)} %bitcast.43, f32[]{:T(128)} %bitcast.42, f32[]{:T(128)} %bitcast.41, f32[]{:T(128)} %bitcast.40, f32[]{:T(128)} %bitcast.39, f32[]{:T(128)} %bitcast.38, f32[]{:T(128)} %bitcast.37, ...), kind=kLoop, calls=%fused_computation.77 | loop fusion | flops 208896 | bytes 417828 | tf_op jit(solution)/shard_map/convert_element_type | solution.py:23
  141.4 5.0 %divide_convert_fusion.14 = bf16[1,4,8,384]{3,2,1,0:T(8,128)(2,1)S(1)} fusion(f32[8,4,8,384]{3,2,1,0:T(8,128)S(1)} %get-tuple-element.45, f32[]{:T(128)S(6)} %max.59, f32[]{:T(128)} %bitcast.68, f32[]{:T(128)} %bitcast.67, f32[]{:T(128)} %bitcast.66, f32[]{:T(128)} %bitcast.65, f32[]{:T(128)} %bitcast.64, f32[]{:T(128)} %bitcast.63, f32[]{:T(128)} %bitcast.62, ...), kind=kLoop, calls=%fused_computation.74 | loop fusion | flops 208896 | bytes 417828 | tf_op jit(solution)/shard_map/convert_element_type | solution.py:23
  146.4 5.0 %divide_convert_fusion.15 = bf16[1,4,8,384]{3,2,1,0:T(8,128)(2,1)S(1)} fusion(f32[8,4,8,384]{3,2,1,0:T(8,128)S(1)} %get-tuple-element.45, f32[]{:T(128)S(6)} %max.58, f32[]{:T(128)} %bitcast.60, f32[]{:T(128)} %bitcast.59, f32[]{:T(128)} %bitcast.58, f32[]{:T(128)} %bitcast.57, f32[]{:T(128)} %bitcast.56, f32[]{:T(128)} %bitcast.55, f32[]{:T(128)} %bitcast.54, ...), kind=kLoop, calls=%fused_computation.75 | loop fusion | flops 208896 | bytes 417828 | tf_op jit(solution)/shard_map/convert_element_type | solution.py:23
  161.5 5.0 %divide_convert_fusion.10 = bf16[1,4,8,384]{3,2,1,0:T(8,128)(2,1)S(1)} fusion(f32[8,4,8,384]{3,2,1,0:T(8,128)S(1)} %get-tuple-element.41, f32[]{:T(128)S(6)} %max.63, f32[]{:T(128)} %bitcast.102, f32[]{:T(128)} %bitcast.101, f32[]{:T(128)} %bitcast.100, f32[]{:T(128)} %bitcast.99, f32[]{:T(128)} %bitcast.98, f32[]{:T(128)} %bitcast.97, f32[]{:T(128)} %bitcast.96, ...), kind=kLoop, calls=%fused_computation.70 | loop fusion | flops 208896 | bytes 417828 | tf_op jit(solution)/shard_map/convert_element_type | solution.py:23
  166.5 5.0 %divide_convert_fusion.11 = bf16[1,4,8,384]{3,2,1,0:T(8,128)(2,1)S(1)} fusion(f32[8,4,8,384]{3,2,1,0:T(8,128)S(1)} %get-tuple-element.41, f32[]{:T(128)S(6)} %max.62, f32[]{:T(128)} %bitcast.94, f32[]{:T(128)} %bitcast.93, f32[]{:T(128)} %bitcast.92, f32[]{:T(128)} %bitcast.91, f32[]{:T(128)} %bitcast.90, f32[]{:T(128)} %bitcast.89, f32[]{:T(128)} %bitcast.88, ...), kind=kLoop, calls=%fused_computation.71 | loop fusion | flops 208896 | bytes 417828 | tf_op jit(solution)/shard_map/convert_element_type | solution.py:23
  171.5 5.1 %divide_convert_fusion.8 = bf16[1,4,8,384]{3,2,1,0:T(8,128)(2,1)S(1)} fusion(f32[8,4,8,384]{3,2,1,0:T(8,128)S(1)} %get-tuple-element.42, f32[]{:T(128)S(6)} %max.65, f32[]{:T(128)} %bitcast.119, f32[]{:T(128)} %bitcast.118, f32[]{:T(128)} %bitcast.117, f32[]{:T(128)} %bitcast.116, f32[]{:T(128)} %bitcast.115, f32[]{:T(128)} %bitcast.114, f32[]{:T(128)} %bitcast.113, ...), kind=kLoop, calls=%fused_computation.68 | loop fusion | flops 208896 | bytes 417828 | tf_op jit(solution)/shard_map/convert_element_type | solution.py:23
  176.6 5.0 %divide_convert_fusion.9 = bf16[1,4,8,384]{3,2,1,0:T(8,128)(2,1)S(1)} fusion(f32[8,4,8,384]{3,2,1,0:T(8,128)S(1)} %get-tuple-element.42, f32[]{:T(128)S(6)} %max.64, f32[]{:T(128)} %bitcast.111, f32[]{:T(128)} %bitcast.110, f32[]{:T(128)} %bitcast.109, f32[]{:T(128)} %bitcast.108, f32[]{:T(128)} %bitcast.107, f32[]{:T(128)} %bitcast.106, f32[]{:T(128)} %bitcast.105, ...), kind=kLoop, calls=%fused_computation.69 | loop fusion | flops 208896 | bytes 417828 | tf_op jit(solution)/shard_map/convert_element_type | solution.py:23
  181.7 4.9 %divide_convert_fusion.6 = bf16[1,4,8,384]{3,2,1,0:T(8,128)(2,1)S(1)} fusion(f32[8,4,8,384]{3,2,1,0:T(8,128)S(1)} %get-tuple-element.43, f32[]{:T(128)S(6)} %max.67, f32[]{:T(128)} %bitcast.136, f32[]{:T(128)} %bitcast.135, f32[]{:T(128)} %bitcast.134, f32[]{:T(128)} %bitcast.133, f32[]{:T(128)} %bitcast.132, f32[]{:T(128)} %bitcast.131, f32[]{:T(128)} %bitcast.130, ...), kind=kLoop, calls=%fused_computation.66 | loop fusion | flops 208896 | bytes 417828 | tf_op jit(solution)/shard_map/convert_element_type | solution.py:23
  186.6 5.0 %divide_convert_fusion.7 = bf16[1,4,8,384]{3,2,1,0:T(8,128)(2,1)S(1)} fusion(f32[8,4,8,384]{3,2,1,0:T(8,128)S(1)} %get-tuple-element.43, f32[]{:T(128)S(6)} %max.66, f32[]{:T(128)} %bitcast.128, f32[]{:T(128)} %bitcast.127, f32[]{:T(128)} %bitcast.126, f32[]{:T(128)} %bitcast.125, f32[]{:T(128)} %bitcast.124, f32[]{:T(128)} %bitcast.123, f32[]{:T(128)} %bitcast.122, ...), kind=kLoop, calls=%fused_computation.67 | loop fusion | flops 208896 | bytes 417828 | tf_op jit(solution)/shard_map/convert_element_type | solution.py:23
  191.7 5.0 %divide_convert_fusion.4 = bf16[1,4,8,384]{3,2,1,0:T(8,128)(2,1)S(1)} fusion(f32[8,4,8,384]{3,2,1,0:T(8,128)S(1)} %get-tuple-element.44, f32[]{:T(128)S(6)} %max.69, f32[]{:T(128)} %bitcast.153, f32[]{:T(128)} %bitcast.152, f32[]{:T(128)} %bitcast.151, f32[]{:T(128)} %bitcast.150, f32[]{:T(128)} %bitcast.149, f32[]{:T(128)} %bitcast.148, f32[]{:T(128)} %bitcast.147, ...), kind=kLoop, calls=%fused_computation.64 | loop fusion | flops 208896 | bytes 417828 | tf_op jit(solution)/shard_map/convert_element_type | solution.py:23
  196.7 4.9 %divide_convert_fusion.5 = bf16[1,4,8,384]{3,2,1,0:T(8,128)(2,1)S(1)} fusion(f32[8,4,8,384]{3,2,1,0:T(8,128)S(1)} %get-tuple-element.44, f32[]{:T(128)S(6)} %max.68, f32[]{:T(128)} %bitcast.145, f32[]{:T(128)} %bitcast.144, f32[]{:T(128)} %bitcast.143, f32[]{:T(128)} %bitcast.142, f32[]{:T(128)} %bitcast.141, f32[]{:T(128)} %bitcast.140, f32[]{:T(128)} %bitcast.139, ...), kind=kLoop, calls=%fused_computation.65 | loop fusion | flops 208896 | bytes 417828 | tf_op jit(solution)/shard_map/convert_element_type | solution.py:23
  201.7 5.0 %divide_convert_fusion.2 = bf16[1,4,8,384]{3,2,1,0:T(8,128)(2,1)S(1)} fusion(f32[8,4,8,384]{3,2,1,0:T(8,128)S(1)} %get-tuple-element.39, f32[]{:T(128)S(6)} %max.71, f32[]{:T(128)} %bitcast.170, f32[]{:T(128)} %bitcast.169, f32[]{:T(128)} %bitcast.168, f32[]{:T(128)} %bitcast.167, f32[]{:T(128)} %bitcast.166, f32[]{:T(128)} %bitcast.165, f32[]{:T(128)} %bitcast.164, ...), kind=kLoop, calls=%fused_computation.62 | loop fusion | flops 208896 | bytes 417828 | tf_op jit(solution)/shard_map/convert_element_type | solution.py:23
  206.7 5.0 %divide_convert_fusion.3 = bf16[1,4,8,384]{3,2,1,0:T(8,128)(2,1)S(1)} fusion(f32[8,4,8,384]{3,2,1,0:T(8,128)S(1)} %get-tuple-element.39, f32[]{:T(128)S(6)} %max.70, f32[]{:T(128)} %bitcast.162, f32[]{:T(128)} %bitcast.161, f32[]{:T(128)} %bitcast.160, f32[]{:T(128)} %bitcast.159, f32[]{:T(128)} %bitcast.158, f32[]{:T(128)} %bitcast.157, f32[]{:T(128)} %bitcast.156, ...), kind=kLoop, calls=%fused_computation.63 | loop fusion | flops 208896 | bytes 417828 | tf_op jit(solution)/shard_map/convert_element_type | solution.py:23
  211.8 10.9 %all_to_all.38 = bf16[8,2,4,8,384]{4,3,2,1,0:T(8,128)(2,1)S(1)} all-to-all(bf16[8,2,4,8,384]{4,3,2,1,0:T(8,128)(2,1)S(1)} %fusion.33), channel_id=1, replica_groups=mesh['rx'=8,'ry'=8,'tp'=4] {'rx'}, dimensions={0} | all-to-all | bytes 786432 | tf_op jit(solution)/shard_map/all_to_all | solution.py:83
  230.7 35.2 %all-to-all-done.6 = bf16[8,8,4,8,384]{4,3,2,1,0:T(8,128)(2,1)S(1)} async-done(((bf16[8,8,4,8,384]{4,3,2,1,0:T(8,128)(2,1)}), bf16[8,8,4,8,384]{4,3,2,1,0:T(8,128)(2,1)S(1)}, u32[]{:S(2)}, u32[]{:S(2)}) %all-to-all-start.6) | async-done | bytes 1572896 | tf_op jit(solution)/shard_map/all_to_all | solution.py:86
  (77 shorter events, 53.8 us)
Async XLA Ops:
  0.6 30.2 %copy-start = (bf16[1,1,512,1536]{3,2,1,0:T(8,128)(2,1)S(1)}, bf16[1,1,512,1536]{3,2,1,0:T(8,128)(2,1)}, u32[]{:S(2)}) copy-start(bf16[1,1,512,1536]{3,2,1,0:T(8,128)(2,1)} %param.6) | copy-start | bytes 4718596
  30.8 29.1 %copy-start.3 = (bf16[4,1,64,1536]{3,2,1,0:T(8,128)(2,1)}, bf16[4,1,64,1536]{3,2,1,0:T(8,128)(2,1)S(1)}, u32[]{:S(2)}) copy-start(bf16[4,1,64,1536]{3,2,1,0:T(8,128)(2,1)S(1)} %get-tuple-element.33) | copy-start | bytes 2359300
  59.9 1.1 copy-start.4
  59.9 1.6 copy-start.7
  63.4 5.9 %copy-start.5 = (s32[8,8]{1,0:T(8,128)S(1)}, s32[8,8]{1,0:T(8,128)}, u32[]{:S(2)}) copy-start(s32[8,8]{1,0:T(8,128)} %param.10) | copy-start | bytes 772
  63.4 5.9 %copy-start.6 = (s32[8,8]{1,0:T(8,128)S(1)}, s32[8,8]{1,0:T(8,128)}, u32[]{:S(2)}) copy-start(s32[8,8]{1,0:T(8,128)} %param.11) | copy-start | bytes 772
  63.4 25.8 %all-to-all-start.3 = ((bf16[8,2,4,8,1536]{4,3,2,1,0:T(8,128)(2,1)}), bf16[8,2,4,8,1536]{4,3,2,1,0:T(8,128)(2,1)S(1)}, u32[]{:S(2)}, u32[]{:S(2)}) async-start(bf16[8,2,4,8,1536]{4,3,2,1,0:T(8,128)(2,1)} %copy_bitcast_fusion), calls=%async_computation.3 | async-start | bytes 3145728 | tf_op jit(solution)/shard_map/all_to_all | solution.py:71
  89.6 1.7 copy-start.1
  104.8 26.5 %all-to-all-start.4 = ((bf16[32,2,8,384]{3,2,1,0:T(8,128)(2,1)}), bf16[32,2,8,384]{3,2,1,0:T(8,128)(2,1)S(1)}, u32[]{:S(2)}, u32[]{:S(2)}) async-start(bf16[32,2,8,384]{3,2,1,0:T(8,128)(2,1)} %bitcast.32), calls=%async_computation.4 | async-start | bytes 786432 | tf_op jit(solution)/shard_map/all_to_all | solution.py:76
  224.1 41.8 %all-to-all-start.6 = ((bf16[8,8,4,8,384]{4,3,2,1,0:T(8,128)(2,1)}), bf16[8,8,4,8,384]{4,3,2,1,0:T(8,128)(2,1)S(1)}, u32[]{:S(2)}, u32[]{:S(2)}) async-start(bf16[8,8,4,8,384]{4,3,2,1,0:T(8,128)(2,1)} %broadcast_select_fusion), calls=%async_computation.6 | async-start | bytes 3145728 | tf_op jit(solution)/shard_map/all_to_all | solution.py:86
  267.0 2.1 copy-start.2

commit v2 on v1

v2 whole, which is shorter than its diff:
```python
import functools

import jax
import jax.numpy as jnp
from jax import lax
from jax.experimental import pallas as pl
from jax.experimental.pallas import tpu as pltpu
from jax.sharding import PartitionSpec as P

learn_rate = 0.5
inv_root_two = 0.7071067811865476
inv_root_tau = 0.3989422804014327

VMEM = pl.BlockSpec(memory_space=pltpu.VMEM)
SMEM = pl.BlockSpec(memory_space=pltpu.SMEM)
ANY = pl.BlockSpec(memory_space=pl.ANY)

TP = 4
SLAB = 16


def call(body, outs, in_specs, out_specs=None, scratch=(), flops=0, name=None):
    many = isinstance(outs, (tuple, list))
    listed = outs if many else (outs,)
    size = sum(o.size * o.dtype.itemsize for o in listed)
    return pl.pallas_call(
        body,
        out_shape=outs,
        in_specs=in_specs,
        out_specs=out_specs if out_specs is not None else ([VMEM] * len(listed) if many else VMEM),
        scratch_shapes=list(scratch),
        compiler_params=pltpu.CompilerParams(vmem_limit_bytes=48 * 2**20),
        cost_estimate=pl.CostEstimate(flops=flops, bytes_accessed=3 * size, transcendentals=0),
        name=name,
    )


def dot(left, right, dims):
    return lax.dot_general(left, right, (dims, ((), ())), preferred_element_type=jnp.float32)


def shape(dims, dtype=jnp.bfloat16):
    return jax.ShapeDtypeStruct(dims, dtype)


def cut_body(t_ref, up_ref, down_ref, *rest):
    outs, sem = rest[:-1], rest[-1]
    t = t_ref[0]
    feat = outs[0].shape[1]
    copies = []
    for n, out in enumerate(outs):
        src = up_ref if n < 3 else down_ref
        r = (2, 3, 1)[n % 3]
        cols = pl.ds(pl.multiple_of((t ^ r) * feat, 128), feat)
        copies.append(pltpu.make_async_copy(src.at[:, cols], out, sem.at[n]))
    for copy in copies:
        copy.start()
    for copy in copies:
        copy.wait()


def part_body(t_ref, x_ref, whole_ref, w1_ref, w2_ref, w3_ref, keep_ref, send_ref, cat):
    rows, feat = w1_ref.shape
    cat[0:rows] = whole_ref[:, pl.ds(pl.multiple_of(t_ref[0] * feat, 128), feat)]
    cat[rows : 2 * rows] = w2_ref[...]
    cat[2 * rows : 3 * rows] = w1_ref[...]
    cat[3 * rows :] = w3_ref[...]
    got = dot(cat[...], x_ref[...], ((1,), (1,)))
    keep_ref[...] = got[: 2 * rows]
    send_ref[...] = got[2 * rows :].astype(jnp.bfloat16)


def step_body(scale, t_ref, own_ref, got_ref, y_ref, whole_ref, w1_ref, w2_ref, w3_ref, out_ref, cat):
    rows, feat = w1_ref.shape
    t = t_ref[0]
    cat[: 2 * rows] = own_ref[...]
    cat[2 * rows :] = got_ref[...]
    half = feat // 2
    base = pl.multiple_of(t * feat, 128)
    for fh in range(2):
        grad = dot(cat[...], y_ref[:, fh * half : (fh + 1) * half], ((1,), (0,)))
        for n, r in enumerate((0, 2, 1, 3)):
            if r == 0:
                old = whole_ref[:, pl.ds(pl.multiple_of(base + fh * half, 128), half)]
            else:
                old = (None, w1_ref, w2_ref, w3_ref)[r][:, fh * half : (fh + 1) * half]
            new = old.astype(jnp.float32) - learn_rate * (grad[n * rows : (n + 1) * rows] * scale)
            new = new.astype(jnp.bfloat16)
            for rb in range(rows // SLAB):
                out_ref[(rb * 2 + fh) * TP + (t ^ r)] = new[rb * SLAB : (rb + 1) * SLAB]


def in_grad_body(scale, t_ref, own_ref, got_ref, whole_ref, w1_ref, w2_ref, w3_ref, out_ref, cat, wcat):
    rows, feat = w1_ref.shape
    cat[: 2 * rows] = own_ref[...]
    cat[2 * rows :] = got_ref[...]
    wcat[0:rows] = whole_ref[:, pl.ds(pl.multiple_of(t_ref[0] * feat, 128), feat)]
    wcat[rows : 2 * rows] = w2_ref[...]
    wcat[2 * rows : 3 * rows] = w1_ref[...]
    wcat[3 * rows :] = w3_ref[...]
    got = dot(cat[...], wcat[...], ((0,), (0,)))
    out_ref[...] = (got * scale).astype(jnp.bfloat16)


def member_scales(labels):
    slots = []
    for slot in range(2):
        member = [jnp.where(label == slot, 1.0, 0.0) for label in labels]
        count = functools.reduce(lambda a, b: a + b, member)
        slots.append((member, jnp.maximum(count, 1.0)))
    return slots


def first_body(n_rx, j_ref, gx_ref, up_ref, down_ref, out_ref):
    j = j_ref[0]
    half = up_ref.shape[2] // 2
    slots = member_scales([gx_ref[j, i] for i in range(n_rx)])
    for u, ref in enumerate((up_ref, down_ref)):
        for tt in range(TP):
            for h in range(2):
                cols = slice(h * half, (h + 1) * half)
                sums = [None, None]
                for i in range(n_rx):
                    term = ref[i * TP + tt, :, cols].astype(jnp.float32)
                    for s in range(2):
                        part = term * slots[s][0][i]
                        sums[s] = part if i == 0 else sums[s] + part
                for s in range(2):
                    out_ref[tt * 2 + h, s, u] = (sums[s] / slots[s][1]).astype(jnp.bfloat16)


def second_body(n_rx, n_ry, gx_ref, gy_ref, z_ref, out_ref, pair):
    def line(i, _):
        slots = member_scales([gy_ref[i, k] for k in range(n_ry)])
        for u in range(2):
            sums = [None, None]
            for k in range(n_ry):
                term = z_ref[k, gx_ref[k, i], u].astype(jnp.float32)
                for s in range(2):
                    part = term * slots[s][0][k]
                    sums[s] = part if k == 0 else sums[s] + part
            for s in range(2):
                pair[s, u] = (sums[s] / slots[s][1]).astype(jnp.bfloat16)
        for k in range(n_ry):
            out_ref[i * n_ry + k] = pair[gy_ref[i, k]]
        return 0

    lax.fori_loop(0, n_rx, line, 0)


def last_body(n_rx, n_ry, f_ref, up_ref, down_ref):
    width = f_ref.shape[3]
    feat = up_ref.shape[1] // TP
    for c in range(n_rx):
        rb, fh = c // 2, c % 2
        for m in range(n_ry):
            tt, h = m // 2, m % 2
            at = tt * feat + fh * (feat // 2) + h * width
            for u, ref in enumerate((up_ref, down_ref)):
                ref[rb * SLAB : (rb + 1) * SLAB, at : at + width] = f_ref[c * n_ry + m, u]


def swap(value, r):
    return lax.ppermute(value, "tp", [(t, t ^ r) for t in range(TP)])


def shards(inputs, out_grads, up_weight, down_weight, group_x, group_y):
    x = inputs[0, 0]
    dy = out_grads[0, 0]
    up = up_weight[0, 0]
    down = down_weight[0, 0]
    tok, feat = x.shape
    rows, width = up.shape
    n_rx = lax.axis_size("rx")
    n_ry = lax.axis_size("ry")
    hid = rows * TP
    scale_in = width ** (-0.5)
    scale_hid = hid ** (-0.5)
    t = lax.axis_index("tp").astype(jnp.int32)[None]
    second_pos = lax.axis_index("ry").astype(jnp.int32)[None]
    flops = 2 * tok * feat * hid

    block = shape((rows, feat))
    cuts = call(cut_body, [block] * 6, [SMEM, ANY, ANY], [ANY] * 6, [pltpu.SemaphoreType.DMA((6,))], name="cut")(t, up, down)
    up2, up3, up1 = (swap(cut, r) for cut, r in zip(cuts[:3], (2, 3, 1)))
    down2, down3, down1 = (swap(cut, r) for cut, r in zip(cuts[3:], (2, 3, 1)))
    ups = (up, up1, up2, up3)
    downs = (down, down1, down2, down3)

    def summed(data, weights, name):
        keep, send = call(
            part_body, [shape((2 * rows, tok), jnp.float32), shape((2 * rows, tok))], [SMEM] + [VMEM] * 5,
            scratch=[pltpu.VMEM((hid, feat), jnp.bfloat16)], flops=flops, name=name,
        )(t, data, *weights)
        both = (keep + swap(send, 1).astype(jnp.float32)).astype(jnp.bfloat16)
        far = swap(both, 2).reshape(2, rows, tok)[::-1].reshape(2 * rows, tok)
        return both.astype(jnp.float32) + far.astype(jnp.float32)

    pre = summed(x, ups, "pre_part") * scale_in
    cdf = 0.5 * (1.0 + lax.erf(pre * inv_root_two))
    act = (pre * cdf).astype(jnp.bfloat16)
    slope = cdf + pre * jnp.exp(-0.5 * pre * pre) * inv_root_tau
    act_got = swap(act, 1)
    pieces = n_rx * TP
    cat = pltpu.VMEM((hid, tok), jnp.bfloat16)

    def stepped(scale, own, got, data, weights, name):
        out = call(
            functools.partial(step_body, scale), shape((pieces, SLAB, feat // 2)), [SMEM] + [VMEM] * 7,
            scratch=[cat], flops=flops, name=name,
        )(t, own, got, data, *weights)
        return lax.all_to_all(out, ("rx", "tp"), 0, 0, tiled=True)

    terms_down = stepped(scale_hid, act, act_got, dy, downs, "step_down")
    hid_grad = summed(dy, downs, "hid_part") * scale_hid
    pre_grad = (hid_grad * slope).astype(jnp.bfloat16)
    pre_grad_got = swap(pre_grad, 1)
    terms_up = stepped(scale_in, pre_grad, pre_grad_got, x, ups, "step_up")
    in_grad = call(
        functools.partial(in_grad_body, scale_in), shape((tok, feat)), [SMEM] + [VMEM] * 6,
        scratch=[cat, pltpu.VMEM((hid, feat), jnp.bfloat16)], flops=flops, name="in_grad",
    )(t, pre_grad, pre_grad_got, *ups)

    mids = call(
        functools.partial(first_body, n_rx), shape((n_ry, 2, 2, SLAB, feat // 4)), [SMEM, SMEM, VMEM, VMEM], name="first_round",
    )(second_pos, group_x, terms_up, terms_down)
    mids = lax.all_to_all(mids, "ry", 0, 0, tiled=True)
    news = call(
        functools.partial(second_body, n_rx, n_ry), shape((n_rx * n_ry, 2, SLAB, feat // 4)), [SMEM, SMEM, VMEM],
        scratch=[pltpu.VMEM((2, 2, SLAB, feat // 4), jnp.bfloat16)], name="second_round",
    )(group_x, group_y, mids)
    news = lax.all_to_all(news, ("rx", "ry"), 0, 0, tiled=True)
    new_up, new_down = call(
        functools.partial(last_body, n_rx, n_ry), [shape((rows, width))] * 2, [VMEM], name="last",
    )(news)
    return (in_grad[None, None], new_up[None, None], new_down[None, None])


def solution(mesh):
    in_specs = (
        P("rx", "ry", None, "tp"),
        P("rx", "ry", None, "tp"),
        P("rx", "ry", "tp", None),
        P("rx", "ry", "tp", None),
        P(),
        P(),
    )
    out_specs = (P("rx", "ry", None, "tp"), P("rx", "ry", "tp", None), P("rx", "ry", "tp", None))
    return jax.shard_map(shards, mesh=mesh, in_specs=in_specs, out_specs=out_specs, check_vma=False)
```

time: 276 us -> 159 us (0.58); the launches traced: 271 us -> 157 us
  other arithmetic: 98.4 us -> 2.65 us
  blocking collectives: 59.4 us -> 22.4 us
  waiting for transfers between devices: 50.8 us -> 75.9 us
  between operations: 12.2 us -> 0.88 us
  starting transfers between devices: 21.2 us -> 30.3 us
  Pallas kernels: 0 us -> 9.05 us
  matrix products: 6.9 us -> 0 us
  local copies, waits for them, and re-layouts: 22.3 us -> 15.8 us
    convert_element_type x22 -> x2, other arithmetic: 92.9 us -> 0.71 us  [summed(): both = (keep + swap(send, 1).astype(jnp.float32)).astype(jnp.bfloat16)]
    all_to_all x4 -> x1, blocking collectives: 59.4 us -> 22.4 us  [shards(): mids = lax.all_to_all(mids, 'ry', 0, 0, tiled=True)]
    ppermute x0 -> x12, waiting for transfers between devices: none -> 17.7 us  [swap(): return lax.ppermute(value, 'tp', [(t, t ^ r) for t in range(TP)])]
    ppermute x0 -> x12, starting transfers between devices: none -> 11.9 us  [swap(): return lax.ppermute(value, 'tp', [(t, t ^ r) for t in range(TP)])]
    slice x15 -> x0, local copies, waits for them, and re-layouts: 10.3 us -> none  [the longest x10 7 us: group_means(): total = sum((terms[k] * member[k] for k in range(terms.shape[0])))]
    unnamed x16 -> x56, local copies, waits for them, and re-layouts: 2.73 us -> 12.6 us
    pallas_call x0 -> x9, Pallas kernels: none -> 9.05 us  [the longest x1 1.77 us: shards(): call(functools.partial(first_body, n_rx), shape((n_ry, 2, 2, SLAB, feat /...]
    another operation x11 -> x0, local copies, waits for them, and re-layouts: 8.1 us -> none  [the longest x2 4.75 us: shards(): both = jnp.stack([up_weight[0, 0], down_weight[0, 0]])]
  transfers between devices with their start and end apart: 3 -> 15, of which waited for: 3 -> 10; matrix products, arithmetic and copies ran while one was open for 4% -> 1% of each run, Pallas kernels for 0% -> 2%
where the time goes in v2:
time: 159 us; the launch traced here: 157 us
  waiting for transfers between devices  75.9 us (48%)
  starting transfers between devices  30.3 us (19%)
  blocking collectives  22.4 us (14%)
  local copies, waits for them, and re-layouts  15.8 us (10%)
  Pallas kernels  9.05 us (6%)
  other arithmetic  2.65 us (2%)
    all_to_all x1, waiting for transfers between devices, shards(): news = lax.all_to_all(news, ('rx', 'ry'), 0, 0, tiled=True)  38.1 us
    all_to_all x1, blocking collectives, shards(): mids = lax.all_to_all(mids, 'ry', 0, 0, tiled=True)  22.4 us
    all_to_all x2, waiting for transfers between devices, stepped(): return lax.all_to_all(out, ('rx', 'tp'), 0, 0, tiled=True)  20.1 us
    ppermute x12, waiting for transfers between devices, swap(): return lax.ppermute(value, 'tp', [(t, t ^ r) for t in range(TP)])  17.7 us
    all_to_all x2, starting transfers between devices, stepped(): return lax.all_to_all(out, ('rx', 'tp'), 0, 0, tiled=True)  13.2 us
    unnamed x56, local copies, waits for them, and re-layouts  12.6 us
    ppermute x12, starting transfers between devices, swap(): return lax.ppermute(value, 'tp', [(t, t ^ r) for t in range(TP)])  11.9 us
    all_to_all x1, starting transfers between devices, shards(): news = lax.all_to_all(news, ('rx', 'ry'), 0, 0, tiled=True)  5.2 us
  transfers between devices with their start and end apart: 15, of which 10 were waited for; matrix products, arithmetic and copies ran while one was open for 1% of the time, Pallas kernels for 2%

profile of v2, /device:TPU:24, one launch (start us, length us, event | category | flops | bytes accessed | tf_op | source)
XLA Modules:
  0.0 156.9 jit_solution(5653530500974622893)
XLA Ops:
  4.6 2.0 %collective-permute-start.2 = (bf16[64,1536]{1,0:T(8,128)(2,1)S(1)}, bf16[64,1536]{1,0:T(8,128)(2,1)S(1)}, u32[]{:S(2)}, u32[]{:S(2)}) collective-permute-start(bf16[64,1536]{1,0:T(8,128)(2,1)S(1)} %get-tuple-element.17), channel_id=1, source_target_pairs={{0,3},{1,2},{2,1},{3,0},{4,7},{5,6},{6,5},{7,4},{8,11},{9,10},{10,... | collective-permute-start | bytes 589832 | tf_op jit(solution)/shard_map/ppermute | solution.py:164
  8.3 1.8 %collective-permute-start.7 = (bf16[64,1536]{1,0:T(8,128)(2,1)S(1)}, bf16[64,1536]{1,0:T(8,128)(2,1)S(1)}, u32[]{:S(2)}, u32[]{:S(2)}) collective-permute-start(bf16[64,1536]{1,0:T(8,128)(2,1)S(1)} %get-tuple-element.22), channel_id=1, source_target_pairs={{0,3},{1,2},{2,1},{3,0},{4,7},{5,6},{6,5},{7,4},{8,11},{9,10},{10,... | collective-permute-start | bytes 589832 | tf_op jit(solution)/shard_map/ppermute | solution.py:164
  10.0 2.6 %collective-permute-done.1.w2_ref = bf16[64,1536]{1,0:T(8,128)(2,1)S(1)} collective-permute-done((bf16[64,1536]{1,0:T(8,128)(2,1)S(1)}, bf16[64,1536]{1,0:T(8,128)(2,1)S(1)}, u32[]{:S(2)}, u32[]{:S(2)}) %collective-permute-start.1) | collective-permute-done | bytes 196640 | tf_op jit(solution)/shard_map/ppermute | solution.py:164
  12.6 3.3 %collective-permute-done.2.w3_ref = bf16[64,1536]{1,0:T(8,128)(2,1)S(1)} collective-permute-done((bf16[64,1536]{1,0:T(8,128)(2,1)S(1)}, bf16[64,1536]{1,0:T(8,128)(2,1)S(1)}, u32[]{:S(2)}, u32[]{:S(2)}) %collective-permute-start.2) | collective-permute-done | bytes 196640 | tf_op jit(solution)/shard_map/ppermute | solution.py:164
  15.9 1.5 copy-done.4
  18.8 2.2 %collective-permute-done.6.w2_ref = bf16[64,1536]{1,0:T(8,128)(2,1)S(1)} collective-permute-done((bf16[64,1536]{1,0:T(8,128)(2,1)S(1)}, bf16[64,1536]{1,0:T(8,128)(2,1)S(1)}, u32[]{:S(2)}, u32[]{:S(2)}) %collective-permute-start.6) | collective-permute-done | bytes 196640 | tf_op jit(solution)/shard_map/ppermute | solution.py:164
  21.0 3.3 %collective-permute-done.7.w3_ref = bf16[64,1536]{1,0:T(8,128)(2,1)S(1)} collective-permute-done((bf16[64,1536]{1,0:T(8,128)(2,1)S(1)}, bf16[64,1536]{1,0:T(8,128)(2,1)S(1)}, u32[]{:S(2)}, u32[]{:S(2)}) %collective-permute-start.7) | collective-permute-done | bytes 196640 | tf_op jit(solution)/shard_map/ppermute | solution.py:164
  27.4 2.3 %collective-permute-start.9 = (bf16[128,512]{1,0:T(8,128)(2,1)}, bf16[128,512]{1,0:T(8,128)(2,1)}, u32[]{:S(2)}, u32[]{:S(2)}) collective-permute-start(bf16[128,512]{1,0:T(8,128)(2,1)} %add_convert_fusion), channel_id=1, source_target_pairs={{0,2},{1,3},{2,0},{3,1},{4,6},{5,7},{6,4},{7,5},{8,10},{9,11},{10,... | collective-permute-start | bytes 393224 | tf_op jit(solution)/shard_map/ppermute | solution.py:164
  29.7 3.6 %collective-permute-done.4 = bf16[128,512]{1,0:T(8,128)(2,1)S(1)} collective-permute-done((bf16[128,512]{1,0:T(8,128)(2,1)S(1)}, bf16[128,512]{1,0:T(8,128)(2,1)S(1)}, u32[]{:S(2)}, u32[]{:S(2)}) %collective-permute-start.4) | collective-permute-done | bytes 131104 | tf_op jit(solution)/shard_map/ppermute | solution.py:164
  33.9 1.6 rev.6
  35.5 1.6 rev.7
  37.1 1.9 %multiply_convert_fusion = (bf16[128,512]{1,0:T(8,128)(2,1)S(1)}, bf16[128,512]{1,0:T(8,128)(2,1)}) fusion(bf16[128,512]{1,0:T(8,128)(2,1)} %add_convert_fusion, bf16[2,64,512]{2,1,0:T(8,128)(2,1)} %rev.7, bf16[2,64,512]{2,1,0:T(8,128)(2,1)} %rev.6, bf16[128,512]{1,0:T(8,128)(2,1)} %copy-done.26), kind=kLoop, calls=%fused_computation.5 | loop fusion | flops 1310720 | bytes 786432 | tf_op jit(solution)/shard_map/convert_element_type | solution.py:201
  39.0 1.3 collective-permute-done.11.got_ref
  44.7 7.5 %all-to-all-start.1 = ((bf16[32,16,768]{2,1,0:T(8,128)(2,1)}), bf16[32,16,768]{2,1,0:T(8,128)(2,1)}, u32[]{:S(2)}, u32[]{:S(2)}) async-start(bf16[32,16,768]{2,1,0:T(8,128)(2,1)} %copy-done.9), calls=%async_computation.1 | async-start | bytes 1572864 | tf_op jit(solution)/shard_map/all_to_all | solution.py:212
  52.4 1.4 collective-permute-done.10.got_ref
  57.8 7.3 %all-to-all-done.1.down_ref = bf16[32,16,768]{2,1,0:T(8,128)(2,1)} async-done(((bf16[32,16,768]{2,1,0:T(8,128)(2,1)}), bf16[32,16,768]{2,1,0:T(8,128)(2,1)}, u32[]{:S(2)}, u32[]{:S(2)}) %all-to-all-start.1) | async-done | bytes 786464 | tf_op jit(solution)/shard_map/all_to_all | solution.py:212
  65.1 5.7 %all-to-all-start = ((bf16[32,16,768]{2,1,0:T(8,128)(2,1)}), bf16[32,16,768]{2,1,0:T(8,128)(2,1)S(1)}, u32[]{:S(2)}, u32[]{:S(2)}) async-start(bf16[32,16,768]{2,1,0:T(8,128)(2,1)} %copy-done.10), calls=%async_computation | async-start | bytes 1572864 | tf_op jit(solution)/shard_map/all_to_all | solution.py:212
  70.8 12.8 %all-to-all-done.up_ref = bf16[32,16,768]{2,1,0:T(8,128)(2,1)S(1)} async-done(((bf16[32,16,768]{2,1,0:T(8,128)(2,1)}), bf16[32,16,768]{2,1,0:T(8,128)(2,1)S(1)}, u32[]{:S(2)}, u32[]{:S(2)}) %all-to-all-start) | async-done | bytes 786464 | tf_op jit(solution)/shard_map/all_to_all | solution.py:212
  83.6 1.8 %first_round.1 = bf16[8,2,2,16,384]{4,3,2,1,0:T(8,128)(2,1)S(1)} custom-call(s32[1]{0:T(128)} %bitcast.10.j_ref, s32[8,8]{1,0:T(8,128)S(1)} %copy-done.24, bf16[32,16,768]{2,1,0:T(8,128)(2,1)S(1)} %all-to-all-done.up_ref, bf16[32,16,768]{2,1,0:T(8,128)(2,1)} %all-to-all-done.1.down_ref), custom_call_target="tpu_custom_call" | custom-call | bytes 1179648 | tf_op jit(solution)/shard_map/first_round/pallas_call | solution.py:224
  85.4 22.4 %all_to_all.20.z_ref = bf16[8,2,2,16,384]{4,3,2,1,0:T(8,128)(2,1)S(1)} all-to-all(bf16[8,2,2,16,384]{4,3,2,1,0:T(8,128)(2,1)S(1)} %first_round.1), channel_id=1, replica_groups=mesh['rx'=8,'ry'=8,'tp'=4] {'ry'}, dimensions={0} | all-to-all | bytes 786432 | tf_op jit(solution)/shard_map/all_to_all | solution.py:227
  107.8 1.6 second_round.1
  110.5 5.2 %all-to-all-start.3 = ((bf16[64,2,16,384]{3,2,1,0:T(8,128)(2,1)}), bf16[64,2,16,384]{3,2,1,0:T(8,128)(2,1)S(1)}, u32[]{:S(2)}, u32[]{:S(2)}) async-start(bf16[64,2,16,384]{3,2,1,0:T(8,128)(2,1)} %copy-done.8), calls=%async_computation.3 | async-start | bytes 3145728 | tf_op jit(solution)/shard_map/all_to_all | solution.py:232
  115.8 1.7 %in_grad.1 = bf16[512,1536]{1,0:T(8,128)(2,1)} custom-call(s32[1]{0:T(128)} %bitcast.t_ref, bf16[128,512]{1,0:T(8,128)(2,1)S(1)} %copy-done.15, bf16[128,512]{1,0:T(8,128)(2,1)S(1)} %copy-done.23, bf16[64,6144]{1,0:T(8,128)(2,1)S(1)} %bitcast.26, bf16[64,1536]{1,0:T(8,128)(2,1)S(1)} %collective-permute-done.5.w1_ref, ...), custom_call_target="tpu_custom_call" | custom-call | flops 402653184 | bytes 4718592 | tf_op jit(solution)/shard_map/in_grad/pallas_call | solution.py:219
  117.5 38.1 %all-to-all-done.3.f_ref = bf16[64,2,16,384]{3,2,1,0:T(8,128)(2,1)S(1)} async-done(((bf16[64,2,16,384]{3,2,1,0:T(8,128)(2,1)}), bf16[64,2,16,384]{3,2,1,0:T(8,128)(2,1)S(1)}, u32[]{:S(2)}, u32[]{:S(2)}) %all-to-all-start.3) | async-done | bytes 1572896 | tf_op jit(solution)/shard_map/all_to_all | solution.py:232
  (77 shorter events, 21.7 us)
Async XLA Ops:
  2.9 12.9 %copy-start.3 = (bf16[1,1,64,6144]{3,2,1,0:T(8,128)(2,1)S(1)}, bf16[1,1,64,6144]{3,2,1,0:T(8,128)(2,1)}, u32[]{:S(2)}) copy-start(bf16[1,1,64,6144]{3,2,1,0:T(8,128)(2,1)} %param.9) | copy-start | bytes 2359300
  3.2 21.1 %copy-start.1 = (bf16[1,1,64,6144]{3,2,1,0:T(8,128)(2,1)S(1)}, bf16[1,1,64,6144]{3,2,1,0:T(8,128)(2,1)}, u32[]{:S(2)}) copy-start(bf16[1,1,64,6144]{3,2,1,0:T(8,128)(2,1)} %param.8) | copy-start | bytes 2359300
  3.2 5.1 %collective-permute-start = (bf16[64,1536]{1,0:T(8,128)(2,1)S(1)}, bf16[64,1536]{1,0:T(8,128)(2,1)S(1)}, u32[]{:S(2)}, u32[]{:S(2)}) collective-permute-start(bf16[64,1536]{1,0:T(8,128)(2,1)S(1)} %get-tuple-element.15), channel_id=1, source_target_pairs={{0,1},{1,0},{2,3},{3,2},{4,5},{5,4},{6,7},{7,6},{8,9},{9,8},{10,11... | collective-permute-start | bytes 589832 | tf_op jit(solution)/shard_map/ppermute | solution.py:164
  3.3 9.3 %collective-permute-start.1 = (bf16[64,1536]{1,0:T(8,128)(2,1)S(1)}, bf16[64,1536]{1,0:T(8,128)(2,1)S(1)}, u32[]{:S(2)}, u32[]{:S(2)}) collective-permute-start(bf16[64,1536]{1,0:T(8,128)(2,1)S(1)} %get-tuple-element.16), channel_id=1, source_target_pairs={{0,2},{1,3},{2,0},{3,1},{4,6},{5,7},{6,4},{7,5},{8,10},{9,11},{10,... | collective-permute-start | bytes 589832 | tf_op jit(solution)/shard_map/ppermute | solution.py:164
  4.6 11.2 %collective-permute-start.2 = (bf16[64,1536]{1,0:T(8,128)(2,1)S(1)}, bf16[64,1536]{1,0:T(8,128)(2,1)S(1)}, u32[]{:S(2)}, u32[]{:S(2)}) collective-permute-start(bf16[64,1536]{1,0:T(8,128)(2,1)S(1)} %get-tuple-element.17), channel_id=1, source_target_pairs={{0,3},{1,2},{2,1},{3,0},{4,7},{5,6},{6,5},{7,4},{8,11},{9,10},{10,... | collective-permute-start | bytes 589832 | tf_op jit(solution)/shard_map/ppermute | solution.py:164
  6.7 12.1 %collective-permute-start.5 = (bf16[64,1536]{1,0:T(8,128)(2,1)S(1)}, bf16[64,1536]{1,0:T(8,128)(2,1)S(1)}, u32[]{:S(2)}, u32[]{:S(2)}) collective-permute-start(bf16[64,1536]{1,0:T(8,128)(2,1)S(1)} %get-tuple-element.20), channel_id=1, source_target_pairs={{0,1},{1,0},{2,3},{3,2},{4,5},{5,4},{6,7},{7,6},{8,9},{9,8},{10,11... | collective-permute-start | bytes 589832 | tf_op jit(solution)/shard_map/ppermute | solution.py:164
  7.0 14.0 %collective-permute-start.6 = (bf16[64,1536]{1,0:T(8,128)(2,1)S(1)}, bf16[64,1536]{1,0:T(8,128)(2,1)S(1)}, u32[]{:S(2)}, u32[]{:S(2)}) collective-permute-start(bf16[64,1536]{1,0:T(8,128)(2,1)S(1)} %get-tuple-element.21), channel_id=1, source_target_pairs={{0,2},{1,3},{2,0},{3,1},{4,6},{5,7},{6,4},{7,5},{8,10},{9,11},{10,... | collective-permute-start | bytes 589832 | tf_op jit(solution)/shard_map/ppermute | solution.py:164
  8.3 16.6 %copy-start.16 = (bf16[64,1536]{1,0:T(8,128)(2,1)}, bf16[64,1536]{1,0:T(8,128)(2,1)S(1)}, u32[]{:S(2)}) copy-start(bf16[64,1536]{1,0:T(8,128)(2,1)S(1)} %collective-permute-done.w1_ref) | copy-start | bytes 589828
  8.3 16.0 %collective-permute-start.7 = (bf16[64,1536]{1,0:T(8,128)(2,1)S(1)}, bf16[64,1536]{1,0:T(8,128)(2,1)S(1)}, u32[]{:S(2)}, u32[]{:S(2)}) collective-permute-start(bf16[64,1536]{1,0:T(8,128)(2,1)S(1)} %get-tuple-element.22), channel_id=1, source_target_pairs={{0,3},{1,2},{2,1},{3,0},{4,7},{5,6},{6,5},{7,4},{8,11},{9,10},{10,... | collective-permute-start | bytes 589832 | tf_op jit(solution)/shard_map/ppermute | solution.py:164
  12.6 12.3 %copy-start.18 = (bf16[64,1536]{1,0:T(8,128)(2,1)}, bf16[64,1536]{1,0:T(8,128)(2,1)S(1)}, u32[]{:S(2)}) copy-start(bf16[64,1536]{1,0:T(8,128)(2,1)S(1)} %collective-permute-done.1.w2_ref) | copy-start | bytes 589828
  15.8 9.1 %copy-start.20 = (bf16[64,1536]{1,0:T(8,128)(2,1)}, bf16[64,1536]{1,0:T(8,128)(2,1)S(1)}, u32[]{:S(2)}) copy-start(bf16[64,1536]{1,0:T(8,128)(2,1)S(1)} %collective-permute-done.2.w3_ref) | copy-start | bytes 589828
  17.9 7.4 %collective-permute-start.3 = (bf16[128,512]{1,0:T(8,128)(2,1)S(1)}, bf16[128,512]{1,0:T(8,128)(2,1)S(1)}, u32[]{:S(2)}, u32[]{:S(2)}) collective-permute-start(bf16[128,512]{1,0:T(8,128)(2,1)S(1)} %get-tuple-element.19), channel_id=1, source_target_pairs={{0,1},{1,0},{2,3},{3,2},{4,5},{5,4},{6,7},{7,6},{8,9},{9,8},{10,11... | collective-permute-start | bytes 393224 | tf_op jit(solution)/shard_map/ppermute | solution.py:164
  24.9 15.4 %copy-start.5 = (bf16[1,1,512,1536]{3,2,1,0:T(8,128)(2,1)S(1)}, bf16[1,1,512,1536]{3,2,1,0:T(8,128)(2,1)}, u32[]{:S(2)}) copy-start(bf16[1,1,512,1536]{3,2,1,0:T(8,128)(2,1)} %param.7) | copy-start | bytes 4718596
  24.9 1.8 %collective-permute-start.8 = (bf16[128,512]{1,0:T(8,128)(2,1)S(1)}, bf16[128,512]{1,0:T(8,128)(2,1)S(1)}, u32[]{:S(2)}, u32[]{:S(2)}) collective-permute-start(bf16[128,512]{1,0:T(8,128)(2,1)S(1)} %get-tuple-element.24), channel_id=1, source_target_pairs={{0,1},{1,0},{2,3},{3,2},{4,5},{5,4},{6,7},{7,6},{8,9},{9,8},{10,11... | collective-permute-start | bytes 393224 | tf_op jit(solution)/shard_map/ppermute | solution.py:164
  25.4 7.9 %collective-permute-start.4 = (bf16[128,512]{1,0:T(8,128)(2,1)S(1)}, bf16[128,512]{1,0:T(8,128)(2,1)S(1)}, u32[]{:S(2)}, u32[]{:S(2)}) collective-permute-start(bf16[128,512]{1,0:T(8,128)(2,1)S(1)} %add_convert_fusion.1), channel_id=1, source_target_pairs={{0,2},{1,3},{2,0},{3,1},{4,6},{5,7},{6,4},{7,5},{8,10},{9,11},{10,... | collective-permute-start | bytes 393224 | tf_op jit(solution)/shard_map/ppermute | solution.py:164
  27.4 8.1 %collective-permute-start.9 = (bf16[128,512]{1,0:T(8,128)(2,1)}, bf16[128,512]{1,0:T(8,128)(2,1)}, u32[]{:S(2)}, u32[]{:S(2)}) collective-permute-start(bf16[128,512]{1,0:T(8,128)(2,1)} %add_convert_fusion), channel_id=1, source_target_pairs={{0,2},{1,3},{2,0},{3,1},{4,6},{5,7},{6,4},{7,5},{8,10},{9,11},{10,... | collective-permute-start | bytes 393224 | tf_op jit(solution)/shard_map/ppermute | solution.py:164
  39.0 1.3 collective-permute-start.11
  44.7 9.2 %copy-start.7 = (bf16[1,1,512,1536]{3,2,1,0:T(8,128)(2,1)S(1)}, bf16[1,1,512,1536]{3,2,1,0:T(8,128)(2,1)}, u32[]{:S(2)}) copy-start(bf16[1,1,512,1536]{3,2,1,0:T(8,128)(2,1)} %param.6) | copy-start | bytes 4718596
  44.7 20.4 %all-to-all-start.1 = ((bf16[32,16,768]{2,1,0:T(8,128)(2,1)}), bf16[32,16,768]{2,1,0:T(8,128)(2,1)}, u32[]{:S(2)}, u32[]{:S(2)}) async-start(bf16[32,16,768]{2,1,0:T(8,128)(2,1)} %copy-done.9), calls=%async_computation.1 | async-start | bytes 1572864 | tf_op jit(solution)/shard_map/all_to_all | solution.py:212
  52.2 1.6 %collective-permute-start.10 = (bf16[128,512]{1,0:T(8,128)(2,1)}, bf16[128,512]{1,0:T(8,128)(2,1)S(1)}, u32[]{:S(2)}, u32[]{:S(2)}) collective-permute-start(bf16[128,512]{1,0:T(8,128)(2,1)} %get-tuple-element.28.own_ref), channel_id=1, source_target_pairs={{0,1},{1,0},{2,3},{3,2},{4,5},{5,4},{6,7},{7,6},{8,9},{9,8},{10,11... | collective-permute-start | bytes 393224 | tf_op jit(solution)/shard_map/ppermute | solution.py:164
  57.8 25.8 %copy-start.24 = (s32[8,8]{1,0:T(8,128)S(1)}, s32[8,8]{1,0:T(8,128)}, u32[]{:S(2)}) copy-start(s32[8,8]{1,0:T(8,128)} %gx_ref.3) | copy-start | bytes 772
  65.1 18.5 %all-to-all-start = ((bf16[32,16,768]{2,1,0:T(8,128)(2,1)}), bf16[32,16,768]{2,1,0:T(8,128)(2,1)S(1)}, u32[]{:S(2)}, u32[]{:S(2)}) async-start(bf16[32,16,768]{2,1,0:T(8,128)(2,1)} %copy-done.10), calls=%async_computation | async-start | bytes 1572864 | tf_op jit(solution)/shard_map/all_to_all | solution.py:212
  70.8 37.0 %copy-start.25 = (s32[8,8]{1,0:T(8,128)S(1)}, s32[8,8]{1,0:T(8,128)}, u32[]{:S(2)}) copy-start(s32[8,8]{1,0:T(8,128)} %gy_ref.1) | copy-start | bytes 772
  110.5 45.1 %all-to-all-start.3 = ((bf16[64,2,16,384]{3,2,1,0:T(8,128)(2,1)}), bf16[64,2,16,384]{3,2,1,0:T(8,128)(2,1)S(1)}, u32[]{:S(2)}, u32[]{:S(2)}) async-start(bf16[64,2,16,384]{3,2,1,0:T(8,128)(2,1)} %copy-done.8), calls=%async_computation.3 | async-start | bytes 3145728 | tf_op jit(solution)/shard_map/all_to_all | solution.py:232
  (19 other events, 38.3 us)

commit v3 on v1

v3 whole, which is shorter than its diff:
```python
import functools

import jax
import jax.numpy as jnp
from jax import lax
from jax.experimental import pallas as pl
from jax.experimental.pallas import tpu as pltpu
from jax.sharding import PartitionSpec as P

learn_rate = 0.5
inv_root_two = 0.7071067811865476
inv_root_tau = 0.3989422804014327

ANY = pl.BlockSpec(memory_space=pl.ANY)
SMEM = pl.BlockSpec(memory_space=pltpu.SMEM)
VMEM = pl.BlockSpec(memory_space=pltpu.VMEM)

TP = 4
SLAB = 16


def shape(dims, dtype=jnp.bfloat16):
    return jax.ShapeDtypeStruct(dims, dtype)


def vmem(dims, dtype=jnp.bfloat16):
    return pltpu.VMEM(dims, dtype)


def call(body, outs, args, specs, scratch=(), out_specs=None, alias=None, flops=0, name=None):
    kinds = {"s": SMEM, "v": VMEM, "a": ANY}
    size = sum(a.size * a.dtype.itemsize for a in list(outs) + list(args))
    return pl.pallas_call(
        body,
        out_shape=list(outs),
        in_specs=[kinds[c] for c in specs],
        out_specs=[kinds[c] for c in out_specs or "v" * len(outs)],
        scratch_shapes=list(scratch),
        input_output_aliases={} if alias is None else {alias: 0},
        compiler_params=pltpu.CompilerParams(vmem_limit_bytes=24 * 2**20),
        cost_estimate=pl.CostEstimate(flops=flops, bytes_accessed=size, transcendentals=0),
        name=name,
    )(*args)


def dot(left, right, dims):
    return lax.dot_general(left, right, (dims, ((), ())), preferred_element_type=jnp.float32)


ORDER = (0, 2, 1, 3)


def cut_body(pos_ref, weight_ref, *rest):
    outs, sems = rest[-5:-1], rest[-1]
    feat = outs[0].shape[1]
    copies = []
    for n, r in enumerate((2, 3, 1, 0)):
        cols = pl.ds(pl.multiple_of((pos_ref[0] ^ r) * feat, 128), feat)
        copies.append(pltpu.make_async_copy(weight_ref.at[:, cols], outs[n], sems.at[n]))
    for copy in copies:
        copy.start()
    for copy in copies:
        copy.wait()


def part_body(x_ref, w0, w1, w2, w3, *rest):
    keep_ref, send_ref, w_ref = rest[-3:]
    rows = w0.shape[0]
    for n, r in enumerate(ORDER):
        w_ref[n * rows : (n + 1) * rows] = (w0, w1, w2, w3)[r][...]
    got = dot(w_ref[...], x_ref[...], ((1,), (1,)))
    half = keep_ref.shape[0]
    keep_ref[...] = got[:half]
    send_ref[...] = got[half:].astype(jnp.bfloat16)


def pair_body(keep_ref, got_ref, both_ref):
    both_ref[...] = (keep_ref[...] + got_ref[...].astype(jnp.float32)).astype(jnp.bfloat16)


def far_sum(both_ref, far_ref):
    rows = both_ref.shape[0] // 2
    far = far_ref[...].astype(jnp.float32)
    return both_ref[...].astype(jnp.float32) + jnp.concatenate([far[rows:], far[:rows]], axis=0)


def act_body(scale, both_ref, far_ref, act_ref, slope_ref):
    pre = far_sum(both_ref, far_ref) * scale
    cdf = 0.5 * (1.0 + lax.erf(pre * inv_root_two))
    act_ref[...] = (pre * cdf).astype(jnp.bfloat16)
    slope_ref[...] = cdf + pre * jnp.exp(-0.5 * pre * pre) * inv_root_tau


def pre_grad_body(scale, both_ref, far_ref, slope_ref, out_ref):
    out_ref[...] = (far_sum(both_ref, far_ref) * scale * slope_ref[...]).astype(jnp.bfloat16)


def step_body(scale, u, pos_ref, own_ref, got_ref, y_ref, w_ref, *rest):
    out_ref, cat, new, sems = rest[-4:]
    half_hid = own_ref.shape[0]
    hid, feat = w_ref.shape
    cat[:half_hid] = own_ref[...]
    cat[half_hid:] = got_ref[...]
    half = feat // 2
    copies = []
    for fh in range(2):
        c = slice(fh * half, (fh + 1) * half)
        grad = dot(cat[...], y_ref[:, c], ((1,), (0,)))
        step = (w_ref[:, c].astype(jnp.float32) - learn_rate * (grad * scale)).astype(jnp.bfloat16)
        new[fh] = step.reshape(new.shape[1:])
        for n, r in enumerate(ORDER):
            copy = pltpu.make_async_copy(new.at[fh, n], out_ref.at[:, fh, pos_ref[0] ^ r, u], sems.at[len(copies)])
            copy.start()
            copies.append(copy)
    for copy in copies:
        copy.wait()


def in_grad_body(scale, own_ref, got_ref, w_ref, out_ref, cat):
    half_hid = own_ref.shape[0]
    cat[:half_hid] = own_ref[...]
    cat[half_hid:] = got_ref[...]
    out_ref[...] = (dot(cat[...], w_ref[...], ((0,), (0,))) * scale).astype(jnp.bfloat16)


def total(values):
    return functools.reduce(lambda a, b: a + b, values)


def members_of(labels):
    members = [[jnp.where(label == s, 1.0, 0.0) for label in labels] for s in range(2)]
    return [(member, jnp.maximum(total(member), 1.0)) for member in members]


def first_body(n_rx, pos_ref, gx_ref, terms_ref, *outs):
    k = pos_ref[2]
    slots = members_of([gx_ref[k, i] for i in range(n_rx)])
    for q, out in enumerate(outs):
        part = lax.rem(k + q, TP)
        for u in range(2):
            values = [terms_ref[i * TP + part, u].astype(jnp.float32) for i in range(n_rx)]
            for s, (member, count) in enumerate(slots):
                out[s, u] = (total(value * one for value, one in zip(values, member)) / count).astype(jnp.bfloat16)


def second_body(u, n_ry, pos_ref, gx_ref, gy_ref, *rest):
    mids, out_ref = rest[:n_ry], rest[-1]
    places = [lax.rem(pos_ref[2] + (n_ry - s), n_ry) for s in range(n_ry)]

    def line(i, _):
        slots = members_of([gy_ref[i, place] for place in places])
        values = [mid[gx_ref[place, i], u].astype(jnp.float32) for mid, place in zip(mids, places)]
        for s, (member, count) in enumerate(slots):
            mean = total(value * one for value, one in zip(values, member)) / count
            out_ref[i, s] = mean.astype(jnp.bfloat16)
        return 0

    lax.fori_loop(0, out_ref.shape[0], line, 0)


def pick_body(n_rx, n_ry, pos_ref, gy_ref, both_ref, *outs):
    i, k = pos_ref[1], pos_ref[2]
    far = jnp.where(lax.rem(k, 2) == 0, n_ry - 2, 2)
    for out, shift in zip(outs, (0, 1, n_ry - 1, far)):
        label = gy_ref[i, lax.rem(k + shift, n_ry)]
        for c in range(n_rx):
            out[c] = both_ref[c, label]


def last_body(n_rx, pos_ref, own_ref, before_ref, after_ref, far_ref, out_ref):
    k = pos_ref[2]
    width = own_ref.shape[2]
    for q, ref in ((0, own_ref), (TP - 1, before_ref), (1, after_ref), (2, far_ref)):
        m = lax.rem(k + q, TP)
        for c in range(n_rx):
            rb, fh = c // 2, c % 2
            cols = pl.ds(pl.multiple_of(m * (2 * width) + fh * width, 128), width)
            out_ref[rb * SLAB : (rb + 1) * SLAB, cols] = ref[c]


def swap(value, r):
    return lax.ppermute(value, "tp", [(t, t ^ r) for t in range(TP)])


def shards(inputs, out_grads, up_weight, down_weight, group_x, group_y):
    x = inputs[0, 0]
    dy = out_grads[0, 0]
    tok, feat = x.shape
    rows, width = up_weight.shape[2:]
    n_rx = lax.axis_size("rx")
    n_ry = lax.axis_size("ry")
    hid = rows * TP
    scale_in = width ** (-0.5)
    scale_hid = hid ** (-0.5)
    pos = jnp.stack([lax.axis_index("tp"), lax.axis_index("rx"), lax.axis_index("ry")]).astype(jnp.int32)
    flops = 2 * tok * feat * hid
    half, half_wide = shape((2 * rows, tok)), shape((2 * rows, tok), jnp.float32)
    cat = vmem((hid, tok))

    def spread(weight, after, name):
        two, three, one, own = call(
            cut_body, [shape((rows, feat))] * TP, [pos, weight, *after], "sa" + "a" * len(after),
            [pltpu.SemaphoreType.DMA((TP,))], "aaaa", name=name,
        )
        two, three, one = swap(two, 2), swap(three, 3), swap(one, 1)
        return [own, one, two, three]

    ups = spread(up_weight[0, 0], [], "cut_up")
    downs = spread(down_weight[0, 0], [ups[1]], "cut_down")

    def summed(data, weights, after, name):
        keep, send, stacked = call(
            part_body, [half_wide, half, shape((hid, feat))], [data, *weights, *after], "vvvvv" + "a" * len(after),
            flops=flops, name="part_" + name,
        )
        (both,) = call(pair_body, [half], [keep, swap(send, 1)], "vv", name="pair_" + name)
        return both, swap(both, 2), stacked

    both, far, up = summed(x, ups, [], "pre")
    act, slope = call(functools.partial(act_body, scale_in), [half, half_wide], [both, far], "vv", name="act")
    act_got = swap(act, 1)
    both, far, down = summed(dy, downs, [both], "hid")
    (pre_grad,) = call(functools.partial(pre_grad_body, scale_hid), [half], [both, far, slope], "vvv", name="pre_grad")
    pre_grad_got = swap(pre_grad, 1)

    def stepped(scale, u, own, got, data, weight, filled, name):
        (out,) = call(
            functools.partial(step_body, scale, u), [shape((n_rx // 2, 2, TP, 2, SLAB, feat // 2))],
            [pos, own, got, data, weight, *filled], "svvvv" + "a" * len(filled),
            [cat, vmem((2, TP, rows // SLAB, SLAB, feat // 2)), pltpu.SemaphoreType.DMA((2 * TP,))], "a",
            alias=5 if filled else None, flops=flops, name=name,
        )
        return out

    steps = stepped(scale_hid, 0, act, act_got, dy, down, [], "step_down")
    steps = stepped(scale_in, 1, pre_grad, pre_grad_got, x, up, [steps], "step_up")
    (in_grad,) = call(
        functools.partial(in_grad_body, scale_in), [shape((tok, feat))], [pre_grad, pre_grad_got, up], "vvv", [cat], flops=flops, name="in_grad"
    )

    terms = lax.all_to_all(steps.reshape(n_rx * TP, 2, SLAB, feat // 2), ("rx", "tp"), 0, 0, tiled=True)
    def along(value, shift):
        return lax.ppermute(value, "ry", [(k, (k + shift) % n_ry) for k in range(n_ry)])

    def two_away(value):
        return lax.ppermute(value, "ry", [(k, (k + (2 if k % 2 else n_ry - 2)) % n_ry) for k in range(n_ry)])

    parts = call(
        functools.partial(first_body, n_rx), [shape((2, 2, SLAB, feat // 2))] * TP, [pos, group_x, terms], "ssv", name="first_round"
    )
    mids = [parts[0]] + [None] * (n_ry - 1)
    for s in (4, 3, 5, 2, 6, 1, 7):
        mids[s] = along(parts[s % TP], s)

    def averaged(u, name):
        (news,) = call(
            functools.partial(second_body, u, n_ry), [shape((n_rx, 2, SLAB, feat // 2))], [pos, group_x, group_y, *mids],
            "sss" + "v" * n_ry, name="second_" + name,
        )
        news = lax.all_to_all(news, "rx", 0, 0, tiled=True)
        own, after, before, far = call(
            functools.partial(pick_body, n_rx, n_ry), [shape((n_rx, SLAB, feat // 2))] * 4, [pos, group_y, news], "ssv", name="pick_" + name
        )
        held = [own, along(after, 1), along(before, -1), two_away(far)]
        (out,) = call(functools.partial(last_body, n_rx), [shape((rows, width))], [pos, *held], "svvvv", name="last_" + name)
        return out

    new_down = averaged(0, "down")
    new_up = averaged(1, "up")
    return (in_grad[None, None], new_up[None, None], new_down[None, None])


def solution(mesh):
    in_specs = (
        P("rx", "ry", None, "tp"),
        P("rx", "ry", None, "tp"),
        P("rx", "ry", "tp", None),
        P("rx", "ry", "tp", None),
        P(),
        P(),
    )
    out_specs = (P("rx", "ry", None, "tp"), P("rx", "ry", "tp", None), P("rx", "ry", "tp", None))
    return jax.shard_map(shards, mesh=mesh, in_specs=in_specs, out_specs=out_specs, check_vma=False)
```

time: 276 us -> 139 us (0.50)
  other arithmetic: 98.4 us -> 0.08 us
  blocking collectives: 59.4 us -> 28.7 us
  starting transfers between devices: 21.2 us -> 50.7 us
  local copies, waits for them, and re-layouts: 22.3 us -> 2.39 us
  Pallas kernels: 0 us -> 18.6 us
  waiting for transfers between devices: 50.8 us -> 34.8 us
  between operations: 12.2 us -> 0.84 us
  matrix products: 6.9 us -> 0 us
    convert_element_type x23 -> x0, other arithmetic: 93 us -> none  [the longest x18 92.2 us: group_means(): (total / jnp.maximum(jnp.sum(member), 1.0)).astype(jnp.bfloat16)]
    all_to_all x3 -> x2, waiting for transfers between devices: 50.8 us -> 4.01 us  [averaged(): news = lax.all_to_all(news, 'rx', 0, 0, tiled=True)]
    ppermute x0 -> x25, starting transfers between devices: none -> 42.5 us  [the longest x11 24.6 us: along(): lax.ppermute(value, 'ry', [(k, (k + shift) % n_ry) for k in range(n_ry)])]
    ppermute x0 -> x25, waiting for transfers between devices: none -> 30.8 us  [the longest x12 16.8 us: swap(): return lax.ppermute(value, 'tp', [(t, t ^ r) for t in range(TP)])]
    all_to_all x4 -> x1, blocking collectives: 59.4 us -> 28.7 us  [shards(): lax.all_to_all(steps.reshape(n_rx * TP, 2, SLAB, feat // 2), ('rx', 'tp')...]
    pallas_call x0 -> x18, Pallas kernels: none -> 18.6 us  [call(): pl.pallas_call(body, out_shape=list(outs), in_specs=[kinds[c] for c in sp...]
    all_to_all x3 -> x2, starting transfers between devices: 21.2 us -> 8.24 us  [averaged(): news = lax.all_to_all(news, 'rx', 0, 0, tiled=True)]
    slice x15 -> x0, local copies, waits for them, and re-layouts: 10.3 us -> none  [the longest x10 7 us: group_means(): total = sum((terms[k] * member[k] for k in range(terms.shape[0])))]
  transfers between devices with their start and end apart: 3 -> 27, of which waited for: 3 -> 15; matrix products, arithmetic and copies ran while one was open for 4% -> 0% of each run, Pallas kernels for 0% -> 8%
where the time goes in v3:
time: 139 us; the launch traced here: 136 us
  starting transfers between devices  50.7 us (36%)
  waiting for transfers between devices  34.8 us (25%)
  blocking collectives  28.7 us (21%)
  Pallas kernels  18.6 us (13%)
  local copies, waits for them, and re-layouts  2.39 us (2%)
    all_to_all x1, blocking collectives, shards(): lax.all_to_all(steps.reshape(n_rx * TP, 2, SLAB, feat // 2), ('rx', 'tp')...  28.7 us
    ppermute x11, starting transfers between devices, along(): lax.ppermute(value, 'ry', [(k, (k + shift) % n_ry) for k in range(n_ry)])  24.6 us
    pallas_call x18, Pallas kernels, call(): pl.pallas_call(body, out_shape=list(outs), in_specs=[kinds[c] for c in sp...  18.6 us
    ppermute x12, waiting for transfers between devices, swap(): return lax.ppermute(value, 'tp', [(t, t ^ r) for t in range(TP)])  16.8 us
    ppermute x12, starting transfers between devices, swap(): return lax.ppermute(value, 'tp', [(t, t ^ r) for t in range(TP)])  12 us
    ppermute x11, waiting for transfers between devices, along(): lax.ppermute(value, 'ry', [(k, (k + shift) % n_ry) for k in range(n_ry)])  11.9 us
    all_to_all x2, starting transfers between devices, averaged(): news = lax.all_to_all(news, 'rx', 0, 0, tiled=True)  8.24 us
    ppermute x2, starting transfers between devices, two_away(): lax.ppermute(value, 'ry', [(k, (k + (2 if k % 2 else n_ry - 2)) % n_ry) f...  5.92 us
  transfers between devices with their start and end apart: 27, of which 15 were waited for; matrix products, arithmetic and copies ran while one was open for 0% of the time, Pallas kernels for 8%

profile of v3, /device:TPU:24, one launch (start us, length us, event | category | flops | bytes accessed | tf_op | source)
XLA Modules:
  0.0 136.2 jit_solution(15669389305533609432)
XLA Ops:
  4.1 2.0 %collective-permute-start.5 = (bf16[64,1536]{1,0:T(8,128)(2,1)S(1)}, bf16[64,1536]{1,0:T(8,128)(2,1)S(1)}, u32[]{:S(2)}, u32[]{:S(2)}) collective-permute-start(bf16[64,1536]{1,0:T(8,128)(2,1)S(1)} %get-tuple-element.38), channel_id=1, source_target_pairs={{0,3},{1,2},{2,1},{3,0},{4,7},{5,6},{6,5},{7,4},{8,11},{9,10},{10,... | collective-permute-start | bytes 589832 | tf_op jit(solution)/shard_map/ppermute | solution.py:182
  12.1 3.3 %collective-permute-done.5.w3 = bf16[64,1536]{1,0:T(8,128)(2,1)S(1)} collective-permute-done((bf16[64,1536]{1,0:T(8,128)(2,1)S(1)}, bf16[64,1536]{1,0:T(8,128)(2,1)S(1)}, u32[]{:S(2)}, u32[]{:S(2)}) %collective-permute-start.5) | collective-permute-done | bytes 196640 | tf_op jit(solution)/shard_map/ppermute | solution.py:182
  17.9 2.7 %collective-permute-done.2.w2 = bf16[64,1536]{1,0:T(8,128)(2,1)S(1)} collective-permute-done((bf16[64,1536]{1,0:T(8,128)(2,1)S(1)}, bf16[64,1536]{1,0:T(8,128)(2,1)S(1)}, u32[]{:S(2)}, u32[]{:S(2)}) %collective-permute-start.2) | collective-permute-done | bytes 196640 | tf_op jit(solution)/shard_map/ppermute | solution.py:182
  20.5 3.3 %collective-permute-done.3.w3 = bf16[64,1536]{1,0:T(8,128)(2,1)S(1)} collective-permute-done((bf16[64,1536]{1,0:T(8,128)(2,1)S(1)}, bf16[64,1536]{1,0:T(8,128)(2,1)S(1)}, u32[]{:S(2)}, u32[]{:S(2)}) %collective-permute-start.3) | collective-permute-done | bytes 196640 | tf_op jit(solution)/shard_map/ppermute | solution.py:182
  26.0 2.4 %collective-permute-start.8 = (bf16[128,512]{1,0:T(8,128)(2,1)S(1)}, bf16[128,512]{1,0:T(8,128)(2,1)S(1)}, u32[]{:S(2)}, u32[]{:S(2)}) collective-permute-start(bf16[128,512]{1,0:T(8,128)(2,1)S(1)} %pair_hid.1.both_ref), channel_id=1, source_target_pairs={{0,2},{1,3},{2,0},{3,1},{4,6},{5,7},{6,4},{7,5},{8,10},{9,11},{10,... | collective-permute-start | bytes 393224 | tf_op jit(solution)/shard_map/ppermute | solution.py:182
  28.4 4.2 %collective-permute-done.9.far_ref = bf16[128,512]{1,0:T(8,128)(2,1)S(1)} collective-permute-done((bf16[128,512]{1,0:T(8,128)(2,1)S(1)}, bf16[128,512]{1,0:T(8,128)(2,1)S(1)}, u32[]{:S(2)}, u32[]{:S(2)}) %collective-permute-start.9) | collective-permute-done | bytes 131104 | tf_op jit(solution)/shard_map/ppermute | solution.py:182
  32.9 1.8 %collective-permute-done.8.far_ref = bf16[128,512]{1,0:T(8,128)(2,1)S(1)} collective-permute-done((bf16[128,512]{1,0:T(8,128)(2,1)S(1)}, bf16[128,512]{1,0:T(8,128)(2,1)S(1)}, u32[]{:S(2)}, u32[]{:S(2)}) %collective-permute-start.8) | collective-permute-done | bytes 131104 | tf_op jit(solution)/shard_map/ppermute | solution.py:182
  38.5 28.7 %all_to_all.15.terms_ref = bf16[32,2,16,768]{3,2,1,0:T(8,128)(2,1)S(1)} all-to-all(bf16[32,2,16,768]{3,2,1,0:T(8,128)(2,1)S(1)} %bitcast.11), channel_id=1, replica_groups=mesh['rx'=8,'ry'=8,'tp'=4] {'rx','tp'}, dimensions={0} | all-to-all | bytes 3145728 | tf_op jit(solution)/shard_map/all_to_all | solution.py:241
  68.4 6.8 %collective-permute-start.16 = (bf16[2,2,16,768]{3,2,1,0:T(8,128)(2,1)S(1)}, bf16[2,2,16,768]{3,2,1,0:T(8,128)(2,1)S(1)}, u32[]{:S(2)}, u32[]{:S(2)}) collective-permute-start(bf16[2,2,16,768]{3,2,1,0:T(8,128)(2,1)S(1)} %get-tuple-element.48), channel_id=1, source_target_pairs={{0,20},{4,24},{8,28},{12,0},{16,4},{20,8},{24,12},{28,16},{1,21},{... | collective-permute-start | bytes 294920 | tf_op jit(solution)/shard_map/ppermute | solution.py:243
  79.2 3.4 %collective-permute-start.18 = (bf16[2,2,16,768]{3,2,1,0:T(8,128)(2,1)S(1)}, bf16[2,2,16,768]{3,2,1,0:T(8,128)(2,1)S(1)}, u32[]{:S(2)}, u32[]{:S(2)}) collective-permute-start(bf16[2,2,16,768]{3,2,1,0:T(8,128)(2,1)S(1)} %get-tuple-element.50), channel_id=1, source_target_pairs={{0,28},{4,0},{8,4},{12,8},{16,12},{20,16},{24,20},{28,24},{1,29},{... | collective-permute-start | bytes 294920 | tf_op jit(solution)/shard_map/ppermute | solution.py:243
  83.1 3.0 %collective-permute-start.14 = (bf16[2,2,16,768]{3,2,1,0:T(8,128)(2,1)S(1)}, bf16[2,2,16,768]{3,2,1,0:T(8,128)(2,1)S(1)}, u32[]{:S(2)}, u32[]{:S(2)}) collective-permute-start(bf16[2,2,16,768]{3,2,1,0:T(8,128)(2,1)S(1)} %get-tuple-element.50), channel_id=1, source_target_pairs={{0,12},{4,16},{8,20},{12,24},{16,28},{20,0},{24,4},{28,8},{1,13},{... | collective-permute-start | bytes 294920 | tf_op jit(solution)/shard_map/ppermute | solution.py:243
  86.9 3.1 %collective-permute-done.18.rest_7_ = bf16[2,2,16,768]{3,2,1,0:T(8,128)(2,1)S(1)} collective-permute-done((bf16[2,2,16,768]{3,2,1,0:T(8,128)(2,1)S(1)}, bf16[2,2,16,768]{3,2,1,0:T(8,128)(2,1)S(1)}, u32[]{:S(2)}, u32[]{:S(2)}) %collective-permute-start.18) | collective-permute-done | bytes 98336 | tf_op jit(solution)/shard_map/ppermute | solution.py:243
  90.0 3.0 %collective-permute-done.14.rest_3_ = bf16[2,2,16,768]{3,2,1,0:T(8,128)(2,1)S(1)} collective-permute-done((bf16[2,2,16,768]{3,2,1,0:T(8,128)(2,1)S(1)}, bf16[2,2,16,768]{3,2,1,0:T(8,128)(2,1)S(1)}, u32[]{:S(2)}, u32[]{:S(2)}) %collective-permute-start.14) | collective-permute-done | bytes 98336 | tf_op jit(solution)/shard_map/ppermute | solution.py:243
  93.0 4.6 %collective-permute-done.15.rest_4_ = bf16[2,2,16,768]{3,2,1,0:T(8,128)(2,1)S(1)} collective-permute-done((bf16[2,2,16,768]{3,2,1,0:T(8,128)(2,1)S(1)}, bf16[2,2,16,768]{3,2,1,0:T(8,128)(2,1)S(1)}, u32[]{:S(2)}, u32[]{:S(2)}) %collective-permute-start.15) | collective-permute-done | bytes 98336 | tf_op jit(solution)/shard_map/ppermute | solution.py:243
  97.6 2.4 %second_down.1 = bf16[8,2,16,768]{3,2,1,0:T(8,128)(2,1)} custom-call(s32[3]{0:T(128)S(1)} %pad_add_fusion.pos_ref, s32[8,8]{1,0:T(8,128)S(1)} %copy-done.5, s32[8,8]{1,0:T(8,128)S(1)} %copy-done.4, bf16[2,2,16,768]{3,2,1,0:T(8,128)(2,1)S(1)} %get-tuple-element.47.rest_0_, bf16[2,2,16,768]{3,2,1,0:T(8,128)(2,1)S(1)} %collective-permute-done.12.rest_1_, ...), custom_call_target="tpu_custom_call" | custom-call | bytes 1180172 | tf_op jit(solution)/shard_map/second_down/pallas_call | solution.py:33
  100.0 3.4 %all-to-all-start.2 = ((bf16[8,2,16,768]{3,2,1,0:T(8,128)(2,1)}), bf16[8,2,16,768]{3,2,1,0:T(8,128)(2,1)S(1)}, u32[]{:S(2)}, u32[]{:S(2)}) async-start(bf16[8,2,16,768]{3,2,1,0:T(8,128)(2,1)} %second_down.1), calls=%async_computation.2 | async-start | bytes 786432 | tf_op jit(solution)/shard_map/all_to_all | solution.py:260
  103.4 2.4 %second_up.1 = bf16[8,2,16,768]{3,2,1,0:T(8,128)(2,1)} custom-call(s32[3]{0:T(128)S(1)} %pad_add_fusion.pos_ref, s32[8,8]{1,0:T(8,128)S(1)} %copy-done.5, s32[8,8]{1,0:T(8,128)S(1)} %copy-done.4, bf16[2,2,16,768]{3,2,1,0:T(8,128)(2,1)S(1)} %get-tuple-element.47.rest_0_, bf16[2,2,16,768]{3,2,1,0:T(8,128)(2,1)S(1)} %collective-permute-done.12.rest_1_, ...), custom_call_target="tpu_custom_call" | custom-call | bytes 1180172 | tf_op jit(solution)/shard_map/second_up/pallas_call | solution.py:33
  105.8 4.0 %all-to-all-done.2.both_ref = bf16[8,2,16,768]{3,2,1,0:T(8,128)(2,1)S(1)} async-done(((bf16[8,2,16,768]{3,2,1,0:T(8,128)(2,1)}), bf16[8,2,16,768]{3,2,1,0:T(8,128)(2,1)S(1)}, u32[]{:S(2)}, u32[]{:S(2)}) %all-to-all-start.2) | async-done | bytes 393248 | tf_op jit(solution)/shard_map/all_to_all | solution.py:260
  109.8 4.8 %all-to-all-start.1 = ((bf16[8,2,16,768]{3,2,1,0:T(8,128)(2,1)}), bf16[8,2,16,768]{3,2,1,0:T(8,128)(2,1)S(1)}, u32[]{:S(2)}, u32[]{:S(2)}) async-start(bf16[8,2,16,768]{3,2,1,0:T(8,128)(2,1)} %second_up.1), calls=%async_computation.1 | async-start | bytes 786432 | tf_op jit(solution)/shard_map/all_to_all | solution.py:260
  115.4 3.2 %collective-permute-start.23 = (bf16[8,16,768]{2,1,0:T(8,128)(2,1)S(1)}, bf16[8,16,768]{2,1,0:T(8,128)(2,1)S(1)}, u32[]{:S(2)}, u32[]{:S(2)}) collective-permute-start(bf16[8,16,768]{2,1,0:T(8,128)(2,1)S(1)} %get-tuple-element.57), channel_id=1, source_target_pairs={{0,28},{4,0},{8,4},{12,8},{16,12},{20,16},{24,20},{28,24},{1,29},{... | collective-permute-start | bytes 589832 | tf_op jit(solution)/shard_map/ppermute | solution.py:243
  118.6 2.8 %collective-permute-start.24 = (bf16[8,16,768]{2,1,0:T(8,128)(2,1)S(1)}, bf16[8,16,768]{2,1,0:T(8,128)(2,1)S(1)}, u32[]{:S(2)}, u32[]{:S(2)}) collective-permute-start(bf16[8,16,768]{2,1,0:T(8,128)(2,1)S(1)} %get-tuple-element.58), channel_id=1, source_target_pairs={{0,24},{4,12},{8,0},{12,20},{16,8},{20,28},{24,16},{28,4},{1,25},{... | collective-permute-start | bytes 589832 | tf_op jit(solution)/shard_map/ppermute | solution.py:246
  122.2 3.2 %collective-permute-start.20 = (bf16[8,16,768]{2,1,0:T(8,128)(2,1)S(1)}, bf16[8,16,768]{2,1,0:T(8,128)(2,1)S(1)}, u32[]{:S(2)}, u32[]{:S(2)}) collective-permute-start(bf16[8,16,768]{2,1,0:T(8,128)(2,1)S(1)} %get-tuple-element.53), channel_id=1, source_target_pairs={{0,28},{4,0},{8,4},{12,8},{16,12},{20,16},{24,20},{28,24},{1,29},{... | collective-permute-start | bytes 589832 | tf_op jit(solution)/shard_map/ppermute | solution.py:243
  125.5 3.1 %collective-permute-start.21 = (bf16[8,16,768]{2,1,0:T(8,128)(2,1)S(1)}, bf16[8,16,768]{2,1,0:T(8,128)(2,1)S(1)}, u32[]{:S(2)}, u32[]{:S(2)}) collective-permute-start(bf16[8,16,768]{2,1,0:T(8,128)(2,1)S(1)} %get-tuple-element.54), channel_id=1, source_target_pairs={{0,24},{4,12},{8,0},{12,20},{16,8},{20,28},{24,16},{28,4},{1,25},{... | collective-permute-start | bytes 589832 | tf_op jit(solution)/shard_map/ppermute | solution.py:246
  132.5 2.2 %collective-permute-done.21.far_ref = bf16[8,16,768]{2,1,0:T(8,128)(2,1)S(1)} collective-permute-done((bf16[8,16,768]{2,1,0:T(8,128)(2,1)S(1)}, bf16[8,16,768]{2,1,0:T(8,128)(2,1)S(1)}, u32[]{:S(2)}, u32[]{:S(2)}) %collective-permute-start.21) | collective-permute-done | bytes 196640 | tf_op jit(solution)/shard_map/ppermute | solution.py:246
  (62 shorter events, 31.4 us)
Async XLA Ops:
  2.7 3.5 %collective-permute-start = (bf16[64,1536]{1,0:T(8,128)(2,1)S(1)}, bf16[64,1536]{1,0:T(8,128)(2,1)S(1)}, u32[]{:S(2)}, u32[]{:S(2)}) collective-permute-start(bf16[64,1536]{1,0:T(8,128)(2,1)S(1)} %get-tuple-element.31), channel_id=1, source_target_pairs={{0,1},{1,0},{2,3},{3,2},{4,5},{5,4},{6,7},{7,6},{8,9},{9,8},{10,11... | collective-permute-start | bytes 589832 | tf_op jit(solution)/shard_map/ppermute | solution.py:182
  2.8 9.3 %collective-permute-start.4 = (bf16[64,1536]{1,0:T(8,128)(2,1)S(1)}, bf16[64,1536]{1,0:T(8,128)(2,1)S(1)}, u32[]{:S(2)}, u32[]{:S(2)}) collective-permute-start(bf16[64,1536]{1,0:T(8,128)(2,1)S(1)} %get-tuple-element.37), channel_id=1, source_target_pairs={{0,2},{1,3},{2,0},{3,1},{4,6},{5,7},{6,4},{7,5},{8,10},{9,11},{10,... | collective-permute-start | bytes 589832 | tf_op jit(solution)/shard_map/ppermute | solution.py:182
  4.1 11.2 %collective-permute-start.5 = (bf16[64,1536]{1,0:T(8,128)(2,1)S(1)}, bf16[64,1536]{1,0:T(8,128)(2,1)S(1)}, u32[]{:S(2)}, u32[]{:S(2)}) collective-permute-start(bf16[64,1536]{1,0:T(8,128)(2,1)S(1)} %get-tuple-element.38), channel_id=1, source_target_pairs={{0,3},{1,2},{2,1},{3,0},{4,7},{5,6},{6,5},{7,4},{8,11},{9,10},{10,... | collective-permute-start | bytes 589832 | tf_op jit(solution)/shard_map/ppermute | solution.py:182
  8.0 9.8 %collective-permute-start.1 = (bf16[64,1536]{1,0:T(8,128)(2,1)S(1)}, bf16[64,1536]{1,0:T(8,128)(2,1)S(1)}, u32[]{:S(2)}, u32[]{:S(2)}) collective-permute-start(bf16[64,1536]{1,0:T(8,128)(2,1)S(1)} %get-tuple-element.33), channel_id=1, source_target_pairs={{0,1},{1,0},{2,3},{3,2},{4,5},{5,4},{6,7},{7,6},{8,9},{9,8},{10,11... | collective-permute-start | bytes 589832 | tf_op jit(solution)/shard_map/ppermute | solution.py:182
  8.5 12.0 %collective-permute-start.2 = (bf16[64,1536]{1,0:T(8,128)(2,1)S(1)}, bf16[64,1536]{1,0:T(8,128)(2,1)S(1)}, u32[]{:S(2)}, u32[]{:S(2)}) collective-permute-start(bf16[64,1536]{1,0:T(8,128)(2,1)S(1)} %get-tuple-element.34), channel_id=1, source_target_pairs={{0,2},{1,3},{2,0},{3,1},{4,6},{5,7},{6,4},{7,5},{8,10},{9,11},{10,... | collective-permute-start | bytes 589832 | tf_op jit(solution)/shard_map/ppermute | solution.py:182
  9.7 14.1 %collective-permute-start.3 = (bf16[64,1536]{1,0:T(8,128)(2,1)S(1)}, bf16[64,1536]{1,0:T(8,128)(2,1)S(1)}, u32[]{:S(2)}, u32[]{:S(2)}) collective-permute-start(bf16[64,1536]{1,0:T(8,128)(2,1)S(1)} %get-tuple-element.35), channel_id=1, source_target_pairs={{0,3},{1,2},{2,1},{3,0},{4,7},{5,6},{6,5},{7,4},{8,11},{9,10},{10,... | collective-permute-start | bytes 589832 | tf_op jit(solution)/shard_map/ppermute | solution.py:182
  24.8 7.8 %collective-permute-start.9 = (bf16[128,512]{1,0:T(8,128)(2,1)S(1)}, bf16[128,512]{1,0:T(8,128)(2,1)S(1)}, u32[]{:S(2)}, u32[]{:S(2)}) collective-permute-start(bf16[128,512]{1,0:T(8,128)(2,1)S(1)} %pair_pre.1.rest_0_.both_ref), channel_id=1, source_target_pairs={{0,2},{1,3},{2,0},{3,1},{4,6},{5,7},{6,4},{7,5},{8,10},{9,11},{10,... | collective-permute-start | bytes 393224 | tf_op jit(solution)/shard_map/ppermute | solution.py:182
  26.0 8.7 %collective-permute-start.8 = (bf16[128,512]{1,0:T(8,128)(2,1)S(1)}, bf16[128,512]{1,0:T(8,128)(2,1)S(1)}, u32[]{:S(2)}, u32[]{:S(2)}) collective-permute-start(bf16[128,512]{1,0:T(8,128)(2,1)S(1)} %pair_hid.1.both_ref), channel_id=1, source_target_pairs={{0,2},{1,3},{2,0},{3,1},{4,6},{5,7},{6,4},{7,5},{8,10},{9,11},{10,... | collective-permute-start | bytes 393224 | tf_op jit(solution)/shard_map/ppermute | solution.py:182
  32.8 2.1 %collective-permute-start.11 = (bf16[128,512]{1,0:T(8,128)(2,1)S(1)}, bf16[128,512]{1,0:T(8,128)(2,1)S(1)}, u32[]{:S(2)}, u32[]{:S(2)}) collective-permute-start(bf16[128,512]{1,0:T(8,128)(2,1)S(1)} %get-tuple-element.45.own_ref), channel_id=1, source_target_pairs={{0,1},{1,0},{2,3},{3,2},{4,5},{5,4},{6,7},{7,6},{8,9},{9,8},{10,11... | collective-permute-start | bytes 393224 | tf_op jit(solution)/shard_map/ppermute | solution.py:182
  68.4 14.6 %collective-permute-start.16 = (bf16[2,2,16,768]{3,2,1,0:T(8,128)(2,1)S(1)}, bf16[2,2,16,768]{3,2,1,0:T(8,128)(2,1)S(1)}, u32[]{:S(2)}, u32[]{:S(2)}) collective-permute-start(bf16[2,2,16,768]{3,2,1,0:T(8,128)(2,1)S(1)} %get-tuple-element.48), channel_id=1, source_target_pairs={{0,20},{4,24},{8,28},{12,0},{16,4},{20,8},{24,12},{28,16},{1,21},{... | collective-permute-start | bytes 294920 | tf_op jit(solution)/shard_map/ppermute | solution.py:243
  75.3 10.9 %collective-permute-start.12 = (bf16[2,2,16,768]{3,2,1,0:T(8,128)(2,1)S(1)}, bf16[2,2,16,768]{3,2,1,0:T(8,128)(2,1)S(1)}, u32[]{:S(2)}, u32[]{:S(2)}) collective-permute-start(bf16[2,2,16,768]{3,2,1,0:T(8,128)(2,1)S(1)} %get-tuple-element.48), channel_id=1, source_target_pairs={{0,4},{4,8},{8,12},{12,16},{16,20},{20,24},{24,28},{28,0},{1,5},{5... | collective-permute-start | bytes 294920 | tf_op jit(solution)/shard_map/ppermute | solution.py:243
  76.3 10.6 %collective-permute-start.17 = (bf16[2,2,16,768]{3,2,1,0:T(8,128)(2,1)S(1)}, bf16[2,2,16,768]{3,2,1,0:T(8,128)(2,1)S(1)}, u32[]{:S(2)}, u32[]{:S(2)}) collective-permute-start(bf16[2,2,16,768]{3,2,1,0:T(8,128)(2,1)S(1)} %get-tuple-element.49), channel_id=1, source_target_pairs={{0,24},{4,28},{8,0},{12,4},{16,8},{20,12},{24,16},{28,20},{1,25},{... | collective-permute-start | bytes 294920 | tf_op jit(solution)/shard_map/ppermute | solution.py:243
  77.7 9.1 %collective-permute-start.13 = (bf16[2,2,16,768]{3,2,1,0:T(8,128)(2,1)S(1)}, bf16[2,2,16,768]{3,2,1,0:T(8,128)(2,1)S(1)}, u32[]{:S(2)}, u32[]{:S(2)}) collective-permute-start(bf16[2,2,16,768]{3,2,1,0:T(8,128)(2,1)S(1)} %get-tuple-element.49), channel_id=1, source_target_pairs={{0,8},{4,12},{8,16},{12,20},{16,24},{20,28},{24,0},{28,4},{1,9},{5... | collective-permute-start | bytes 294920 | tf_op jit(solution)/shard_map/ppermute | solution.py:243
  79.2 10.8 %collective-permute-start.18 = (bf16[2,2,16,768]{3,2,1,0:T(8,128)(2,1)S(1)}, bf16[2,2,16,768]{3,2,1,0:T(8,128)(2,1)S(1)}, u32[]{:S(2)}, u32[]{:S(2)}) collective-permute-start(bf16[2,2,16,768]{3,2,1,0:T(8,128)(2,1)S(1)} %get-tuple-element.50), channel_id=1, source_target_pairs={{0,28},{4,0},{8,4},{12,8},{16,12},{20,16},{24,20},{28,24},{1,29},{... | collective-permute-start | bytes 294920 | tf_op jit(solution)/shard_map/ppermute | solution.py:243
  83.1 9.9 %collective-permute-start.14 = (bf16[2,2,16,768]{3,2,1,0:T(8,128)(2,1)S(1)}, bf16[2,2,16,768]{3,2,1,0:T(8,128)(2,1)S(1)}, u32[]{:S(2)}, u32[]{:S(2)}) collective-permute-start(bf16[2,2,16,768]{3,2,1,0:T(8,128)(2,1)S(1)} %get-tuple-element.50), channel_id=1, source_target_pairs={{0,12},{4,16},{8,20},{12,24},{16,28},{20,0},{24,4},{28,8},{1,13},{... | collective-permute-start | bytes 294920 | tf_op jit(solution)/shard_map/ppermute | solution.py:243
  86.1 11.5 %collective-permute-start.15 = (bf16[2,2,16,768]{3,2,1,0:T(8,128)(2,1)S(1)}, bf16[2,2,16,768]{3,2,1,0:T(8,128)(2,1)S(1)}, u32[]{:S(2)}, u32[]{:S(2)}) collective-permute-start(bf16[2,2,16,768]{3,2,1,0:T(8,128)(2,1)S(1)} %get-tuple-element.47.rest_0_), channel_id=1, source_target_pairs={{0,16},{4,20},{8,24},{12,28},{16,0},{20,4},{24,8},{28,12},{1,17},{... | collective-permute-start | bytes 294920 | tf_op jit(solution)/shard_map/ppermute | solution.py:243
  100.0 9.8 %all-to-all-start.2 = ((bf16[8,2,16,768]{3,2,1,0:T(8,128)(2,1)}), bf16[8,2,16,768]{3,2,1,0:T(8,128)(2,1)S(1)}, u32[]{:S(2)}, u32[]{:S(2)}) async-start(bf16[8,2,16,768]{3,2,1,0:T(8,128)(2,1)} %second_down.1), calls=%async_computation.2 | async-start | bytes 786432 | tf_op jit(solution)/shard_map/all_to_all | solution.py:260
  109.8 11.7 %all-to-all-start.1 = ((bf16[8,2,16,768]{3,2,1,0:T(8,128)(2,1)}), bf16[8,2,16,768]{3,2,1,0:T(8,128)(2,1)S(1)}, u32[]{:S(2)}, u32[]{:S(2)}) async-start(bf16[8,2,16,768]{3,2,1,0:T(8,128)(2,1)} %second_up.1), calls=%async_computation.1 | async-start | bytes 786432 | tf_op jit(solution)/shard_map/all_to_all | solution.py:260
  115.3 10.2 %collective-permute-start.22 = (bf16[8,16,768]{2,1,0:T(8,128)(2,1)S(1)}, bf16[8,16,768]{2,1,0:T(8,128)(2,1)S(1)}, u32[]{:S(2)}, u32[]{:S(2)}) collective-permute-start(bf16[8,16,768]{2,1,0:T(8,128)(2,1)S(1)} %get-tuple-element.56), channel_id=1, source_target_pairs={{0,4},{4,8},{8,12},{12,16},{16,20},{20,24},{24,28},{28,0},{1,5},{5... | collective-permute-start | bytes 589832 | tf_op jit(solution)/shard_map/ppermute | solution.py:243
  115.4 14.9 %collective-permute-start.23 = (bf16[8,16,768]{2,1,0:T(8,128)(2,1)S(1)}, bf16[8,16,768]{2,1,0:T(8,128)(2,1)S(1)}, u32[]{:S(2)}, u32[]{:S(2)}) collective-permute-start(bf16[8,16,768]{2,1,0:T(8,128)(2,1)S(1)} %get-tuple-element.57), channel_id=1, source_target_pairs={{0,28},{4,0},{8,4},{12,8},{16,12},{20,16},{24,20},{28,24},{1,29},{... | collective-permute-start | bytes 589832 | tf_op jit(solution)/shard_map/ppermute | solution.py:243
  118.6 11.7 %collective-permute-start.24 = (bf16[8,16,768]{2,1,0:T(8,128)(2,1)S(1)}, bf16[8,16,768]{2,1,0:T(8,128)(2,1)S(1)}, u32[]{:S(2)}, u32[]{:S(2)}) collective-permute-start(bf16[8,16,768]{2,1,0:T(8,128)(2,1)S(1)} %get-tuple-element.58), channel_id=1, source_target_pairs={{0,24},{4,12},{8,0},{12,20},{16,8},{20,28},{24,16},{28,4},{1,25},{... | collective-permute-start | bytes 589832 | tf_op jit(solution)/shard_map/ppermute | solution.py:246
  122.2 9.9 %collective-permute-start.19 = (bf16[8,16,768]{2,1,0:T(8,128)(2,1)S(1)}, bf16[8,16,768]{2,1,0:T(8,128)(2,1)S(1)}, u32[]{:S(2)}, u32[]{:S(2)}) collective-permute-start(bf16[8,16,768]{2,1,0:T(8,128)(2,1)S(1)} %get-tuple-element.52), channel_id=1, source_target_pairs={{0,4},{4,8},{8,12},{12,16},{16,20},{20,24},{24,28},{28,0},{1,5},{5... | collective-permute-start | bytes 589832 | tf_op jit(solution)/shard_map/ppermute | solution.py:243
  122.2 10.3 %collective-permute-start.20 = (bf16[8,16,768]{2,1,0:T(8,128)(2,1)S(1)}, bf16[8,16,768]{2,1,0:T(8,128)(2,1)S(1)}, u32[]{:S(2)}, u32[]{:S(2)}) collective-permute-start(bf16[8,16,768]{2,1,0:T(8,128)(2,1)S(1)} %get-tuple-element.53), channel_id=1, source_target_pairs={{0,28},{4,0},{8,4},{12,8},{16,12},{20,16},{24,20},{28,24},{1,29},{... | collective-permute-start | bytes 589832 | tf_op jit(solution)/shard_map/ppermute | solution.py:243
  125.5 9.2 %collective-permute-start.21 = (bf16[8,16,768]{2,1,0:T(8,128)(2,1)S(1)}, bf16[8,16,768]{2,1,0:T(8,128)(2,1)S(1)}, u32[]{:S(2)}, u32[]{:S(2)}) collective-permute-start(bf16[8,16,768]{2,1,0:T(8,128)(2,1)S(1)} %get-tuple-element.54), channel_id=1, source_target_pairs={{0,24},{4,12},{8,0},{12,20},{16,8},{20,28},{24,16},{28,4},{1,25},{... | collective-permute-start | bytes 589832 | tf_op jit(solution)/shard_map/ppermute | solution.py:246
  (9 other events, 97.3 us)

commit v4 on v3

--- a/solution.py
+++ b/solution.py
@@ -16,6 +16,7 @@
 VMEM = pl.BlockSpec(memory_space=pltpu.VMEM)
 
 TP = 4
+SHIFTS = (0, 1, 7, 2, 6, 3, 5, 4)
 SLAB = 16
 
 
@@ -129,30 +130,38 @@
 
 def members_of(labels):
     members = [[jnp.where(label == s, 1.0, 0.0) for label in labels] for s in range(2)]
-    return [(member, jnp.maximum(total(member), 1.0)) for member in members]
+    return [(member, 1.0 / jnp.maximum(total(member), 1.0)) for member in members]
+
+
+def group_means(terms, slots):
+    sums = [None, None]
+    for n, term in enumerate(terms):
+        term = term.astype(jnp.float32)
+        for s, (member, _) in enumerate(slots):
+            part = term * member[n]
+            sums[s] = part if n == 0 else sums[s] + part
+    return [(value * share).astype(jnp.bfloat16) for value, (_, share) in zip(sums, slots)]
 
 
 def first_body(n_rx, pos_ref, gx_ref, terms_ref, *outs):
     k = pos_ref[2]
     slots = members_of([gx_ref[k, i] for i in range(n_rx)])
-    for q, out in enumerate(outs):
+    for q in range(TP):
         part = lax.rem(k + q, TP)
         for u in range(2):
-            values = [terms_ref[i * TP + part, u].astype(jnp.float32) for i in range(n_rx)]
-            for s, (member, count) in enumerate(slots):
-                out[s, u] = (total(value * one for value, one in zip(values, member)) / count).astype(jnp.bfloat16)
+            for s, mean in enumerate(group_means((terms_ref[i * TP + part, u] for i in range(n_rx)), slots)):
+                for shift in range(q, len(outs), TP):
+                    outs[SHIFTS.index(shift)][s, u] = mean
 
 
 def second_body(u, n_ry, pos_ref, gx_ref, gy_ref, *rest):
     mids, out_ref = rest[:n_ry], rest[-1]
-    places = [lax.rem(pos_ref[2] + (n_ry - s), n_ry) for s in range(n_ry)]
+    places = [lax.rem(pos_ref[2] + (n_ry - s), n_ry) for s in SHIFTS]
 
     def line(i, _):
         slots = members_of([gy_ref[i, place] for place in places])
-        values = [mid[gx_ref[place, i], u].astype(jnp.float32) for mid, place in zip(mids, places)]
-        for s, (member, count) in enumerate(slots):
-            mean = total(value * one for value, one in zip(values, member)) / count
-            out_ref[i, s] = mean.astype(jnp.bfloat16)
+        for s, mean in enumerate(group_means((mid[gx_ref[place, i], u] for mid, place in zip(mids, places)), slots)):
+            out_ref[i, s] = mean
         return 0
 
     lax.fori_loop(0, out_ref.shape[0], line, 0)
@@ -246,11 +255,9 @@
         return lax.ppermute(value, "ry", [(k, (k + (2 if k % 2 else n_ry - 2)) % n_ry) for k in range(n_ry)])
 
     parts = call(
-        functools.partial(first_body, n_rx), [shape((2, 2, SLAB, feat // 2))] * TP, [pos, group_x, terms], "ssv", name="first_round"
+        functools.partial(first_body, n_rx), [shape((2, 2, SLAB, feat // 2))] * n_ry, [pos, group_x, terms], "ssv", name="first_round"
     )
-    mids = [parts[0]] + [None] * (n_ry - 1)
-    for s in (4, 3, 5, 2, 6, 1, 7):
-        mids[s] = along(parts[s % TP], s)
+    mids = [along(part, s) if s else part for s, part in zip(SHIFTS, parts)]
 
     def averaged(u, name):
         (news,) = call(

time: 139 us -> 137 us (0.986); the launches traced: 136 us -> 137 us
  starting transfers between devices: 50.7 us -> 53.7 us
  waiting for transfers between devices: 34.8 us -> 32.5 us
    ppermute x11, starting transfers between devices: 24.6 us -> 29.2 us  [along(): lax.ppermute(value, 'ry', [(k, (k + shift) % n_ry) for k in range(n_ry)])]
    ppermute x2, waiting for transfers between devices: 2.16 us -> 0.01 us  [two_away(): lax.ppermute(value, 'ry', [(k, (k + (2 if k % 2 else n_ry - 2)) % n_ry) f...]
    ppermute x2, starting transfers between devices: 5.92 us -> 3.93 us  [two_away(): lax.ppermute(value, 'ry', [(k, (k + (2 if k % 2 else n_ry - 2)) % n_ry) f...]
  transfers between devices with their start and end apart: 27 -> 27, of which waited for: 15 -> 13; matrix products, arithmetic and copies ran while one was open for 0% -> 0% of each run, Pallas kernels for 8% -> 8%
where the time goes in v4:
time: 137 us
  starting transfers between devices  53.7 us (39%)
  waiting for transfers between devices  32.5 us (24%)
  blocking collectives  28.7 us (21%)
  Pallas kernels  18.4 us (13%)
  local copies, waits for them, and re-layouts  2.39 us (2%)
    ppermute x11, starting transfers between devices, along(): lax.ppermute(value, 'ry', [(k, (k + shift) % n_ry) for k in range(n_ry)])  29.2 us
    all_to_all x1, blocking collectives, shards(): lax.all_to_all(steps.reshape(n_rx * TP, 2, SLAB, feat // 2), ('rx', 'tp')...  28.7 us
    pallas_call x18, Pallas kernels, call(): pl.pallas_call(body, out_shape=list(outs), in_specs=[kinds[c] for c in sp...  18.4 us
    ppermute x12, waiting for transfers between devices, swap(): return lax.ppermute(value, 'tp', [(t, t ^ r) for t in range(TP)])  16.8 us
    ppermute x12, starting transfers between devices, swap(): return lax.ppermute(value, 'tp', [(t, t ^ r) for t in range(TP)])  12 us
    ppermute x11, waiting for transfers between devices, along(): lax.ppermute(value, 'ry', [(k, (k + shift) % n_ry) for k in range(n_ry)])  11.6 us
    all_to_all x2, starting transfers between devices, averaged(): news = lax.all_to_all(news, 'rx', 0, 0, tiled=True)  8.67 us
    all_to_all x2, waiting for transfers between devices, averaged(): news = lax.all_to_all(news, 'rx', 0, 0, tiled=True)  4.18 us
  transfers between devices with their start and end apart: 27, of which 13 were waited for; matrix products, arithmetic and copies ran while one was open for 0% of the time, Pallas kernels for 8%

profile of v4, /device:TPU:24, one launch (start us, length us, event | category | flops | bytes accessed | tf_op | source)
XLA Modules:
  0.0 136.7 jit_solution(5811364310147210349)
XLA Ops:
  4.1 2.0 %collective-permute-start.5 = (bf16[64,1536]{1,0:T(8,128)(2,1)S(1)}, bf16[64,1536]{1,0:T(8,128)(2,1)S(1)}, u32[]{:S(2)}, u32[]{:S(2)}) collective-permute-start(bf16[64,1536]{1,0:T(8,128)(2,1)S(1)} %get-tuple-element.42), channel_id=1, source_target_pairs={{0,3},{1,2},{2,1},{3,0},{4,7},{5,6},{6,5},{7,4},{8,11},{9,10},{10,... | collective-permute-start | bytes 589832 | tf_op jit(solution)/shard_map/ppermute | solution.py:191
  12.1 3.3 %collective-permute-done.5.w3 = bf16[64,1536]{1,0:T(8,128)(2,1)S(1)} collective-permute-done((bf16[64,1536]{1,0:T(8,128)(2,1)S(1)}, bf16[64,1536]{1,0:T(8,128)(2,1)S(1)}, u32[]{:S(2)}, u32[]{:S(2)}) %collective-permute-start.5) | collective-permute-done | bytes 196640 | tf_op jit(solution)/shard_map/ppermute | solution.py:191
  17.9 2.7 %collective-permute-done.2.w2 = bf16[64,1536]{1,0:T(8,128)(2,1)S(1)} collective-permute-done((bf16[64,1536]{1,0:T(8,128)(2,1)S(1)}, bf16[64,1536]{1,0:T(8,128)(2,1)S(1)}, u32[]{:S(2)}, u32[]{:S(2)}) %collective-permute-start.2) | collective-permute-done | bytes 196640 | tf_op jit(solution)/shard_map/ppermute | solution.py:191
  20.5 3.3 %collective-permute-done.3.w3 = bf16[64,1536]{1,0:T(8,128)(2,1)S(1)} collective-permute-done((bf16[64,1536]{1,0:T(8,128)(2,1)S(1)}, bf16[64,1536]{1,0:T(8,128)(2,1)S(1)}, u32[]{:S(2)}, u32[]{:S(2)}) %collective-permute-start.3) | collective-permute-done | bytes 196640 | tf_op jit(solution)/shard_map/ppermute | solution.py:191
  26.0 2.4 %collective-permute-start.8 = (bf16[128,512]{1,0:T(8,128)(2,1)S(1)}, bf16[128,512]{1,0:T(8,128)(2,1)S(1)}, u32[]{:S(2)}, u32[]{:S(2)}) collective-permute-start(bf16[128,512]{1,0:T(8,128)(2,1)S(1)} %pair_hid.1.both_ref), channel_id=1, source_target_pairs={{0,2},{1,3},{2,0},{3,1},{4,6},{5,7},{6,4},{7,5},{8,10},{9,11},{10,... | collective-permute-start | bytes 393224 | tf_op jit(solution)/shard_map/ppermute | solution.py:191
  28.4 4.2 %collective-permute-done.9.far_ref = bf16[128,512]{1,0:T(8,128)(2,1)S(1)} collective-permute-done((bf16[128,512]{1,0:T(8,128)(2,1)S(1)}, bf16[128,512]{1,0:T(8,128)(2,1)S(1)}, u32[]{:S(2)}, u32[]{:S(2)}) %collective-permute-start.9) | collective-permute-done | bytes 131104 | tf_op jit(solution)/shard_map/ppermute | solution.py:191
  38.5 28.7 %all_to_all.15.terms_ref = bf16[32,2,16,768]{3,2,1,0:T(8,128)(2,1)S(1)} all-to-all(bf16[32,2,16,768]{3,2,1,0:T(8,128)(2,1)S(1)} %bitcast.11), channel_id=1, replica_groups=mesh['rx'=8,'ry'=8,'tp'=4] {'rx','tp'}, dimensions={0} | all-to-all | bytes 3145728 | tf_op jit(solution)/shard_map/all_to_all | solution.py:250
  68.4 2.0 %collective-permute-start.12 = (bf16[2,2,16,768]{3,2,1,0:T(8,128)(2,1)S(1)}, bf16[2,2,16,768]{3,2,1,0:T(8,128)(2,1)S(1)}, u32[]{:S(2)}, u32[]{:S(2)}) collective-permute-start(bf16[2,2,16,768]{3,2,1,0:T(8,128)(2,1)S(1)} %get-tuple-element.52), channel_id=1, source_target_pairs={{0,4},{4,8},{8,12},{12,16},{16,20},{20,24},{24,28},{28,0},{1,5},{5... | collective-permute-start | bytes 294920 | tf_op jit(solution)/shard_map/ppermute | solution.py:252
  70.3 4.0 %collective-permute-start.13 = (bf16[2,2,16,768]{3,2,1,0:T(8,128)(2,1)S(1)}, bf16[2,2,16,768]{3,2,1,0:T(8,128)(2,1)S(1)}, u32[]{:S(2)}, u32[]{:S(2)}) collective-permute-start(bf16[2,2,16,768]{3,2,1,0:T(8,128)(2,1)S(1)} %get-tuple-element.53), channel_id=1, source_target_pairs={{0,28},{4,0},{8,4},{12,8},{16,12},{20,16},{24,20},{28,24},{1,29},{... | collective-permute-start | bytes 294920 | tf_op jit(solution)/shard_map/ppermute | solution.py:252
  74.4 4.1 %collective-permute-start.15 = (bf16[2,2,16,768]{3,2,1,0:T(8,128)(2,1)S(1)}, bf16[2,2,16,768]{3,2,1,0:T(8,128)(2,1)S(1)}, u32[]{:S(2)}, u32[]{:S(2)}) collective-permute-start(bf16[2,2,16,768]{3,2,1,0:T(8,128)(2,1)S(1)} %get-tuple-element.55), channel_id=1, source_target_pairs={{0,24},{4,28},{8,0},{12,4},{16,8},{20,12},{24,16},{28,20},{1,25},{... | collective-permute-start | bytes 294920 | tf_op jit(solution)/shard_map/ppermute | solution.py:252
  79.1 4.4 %collective-permute-start.17 = (bf16[2,2,16,768]{3,2,1,0:T(8,128)(2,1)S(1)}, bf16[2,2,16,768]{3,2,1,0:T(8,128)(2,1)S(1)}, u32[]{:S(2)}, u32[]{:S(2)}) collective-permute-start(bf16[2,2,16,768]{3,2,1,0:T(8,128)(2,1)S(1)} %get-tuple-element.57), channel_id=1, source_target_pairs={{0,20},{4,24},{8,28},{12,0},{16,4},{20,8},{24,12},{28,16},{1,21},{... | collective-permute-start | bytes 294920 | tf_op jit(solution)/shard_map/ppermute | solution.py:252
  83.6 4.5 %collective-permute-start.18 = (bf16[2,2,16,768]{3,2,1,0:T(8,128)(2,1)S(1)}, bf16[2,2,16,768]{3,2,1,0:T(8,128)(2,1)S(1)}, u32[]{:S(2)}, u32[]{:S(2)}) collective-permute-start(bf16[2,2,16,768]{3,2,1,0:T(8,128)(2,1)S(1)} %get-tuple-element.58), channel_id=1, source_target_pairs={{0,16},{4,20},{8,24},{12,28},{16,0},{20,4},{24,8},{28,12},{1,17},{... | collective-permute-start | bytes 294920 | tf_op jit(solution)/shard_map/ppermute | solution.py:252
  88.0 2.6 %collective-permute-done.16.rest_5_ = bf16[2,2,16,768]{3,2,1,0:T(8,128)(2,1)S(1)} collective-permute-done((bf16[2,2,16,768]{3,2,1,0:T(8,128)(2,1)S(1)}, bf16[2,2,16,768]{3,2,1,0:T(8,128)(2,1)S(1)}, u32[]{:S(2)}, u32[]{:S(2)}) %collective-permute-start.16) | collective-permute-done | bytes 98336 | tf_op jit(solution)/shard_map/ppermute | solution.py:252
  90.7 2.8 %collective-permute-done.17.rest_6_ = bf16[2,2,16,768]{3,2,1,0:T(8,128)(2,1)S(1)} collective-permute-done((bf16[2,2,16,768]{3,2,1,0:T(8,128)(2,1)S(1)}, bf16[2,2,16,768]{3,2,1,0:T(8,128)(2,1)S(1)}, u32[]{:S(2)}, u32[]{:S(2)}) %collective-permute-start.17) | collective-permute-done | bytes 98336 | tf_op jit(solution)/shard_map/ppermute | solution.py:252
  93.6 2.3 %second_down.1 = bf16[8,2,16,768]{3,2,1,0:T(8,128)(2,1)} custom-call(s32[3]{0:T(128)S(1)} %pad_add_fusion.pos_ref, s32[8,8]{1,0:T(8,128)S(1)} %copy-done.5, s32[8,8]{1,0:T(8,128)S(1)} %copy-done.4, bf16[2,2,16,768]{3,2,1,0:T(8,128)(2,1)S(1)} %get-tuple-element.51.rest_0_, bf16[2,2,16,768]{3,2,1,0:T(8,128)(2,1)S(1)} %collective-permute-done.12.rest_1_, ...), custom_call_target="tpu_custom_call" | custom-call | bytes 1180172 | tf_op jit(solution)/shard_map/second_down/pallas_call | solution.py:34
  96.0 3.8 %all-to-all-start.2 = ((bf16[8,2,16,768]{3,2,1,0:T(8,128)(2,1)}), bf16[8,2,16,768]{3,2,1,0:T(8,128)(2,1)S(1)}, u32[]{:S(2)}, u32[]{:S(2)}) async-start(bf16[8,2,16,768]{3,2,1,0:T(8,128)(2,1)} %second_down.1), calls=%async_computation.2 | async-start | bytes 786432 | tf_op jit(solution)/shard_map/all_to_all | solution.py:267
  99.8 2.3 %second_up.1 = bf16[8,2,16,768]{3,2,1,0:T(8,128)(2,1)} custom-call(s32[3]{0:T(128)S(1)} %pad_add_fusion.pos_ref, s32[8,8]{1,0:T(8,128)S(1)} %copy-done.5, s32[8,8]{1,0:T(8,128)S(1)} %copy-done.4, bf16[2,2,16,768]{3,2,1,0:T(8,128)(2,1)S(1)} %get-tuple-element.51.rest_0_, bf16[2,2,16,768]{3,2,1,0:T(8,128)(2,1)S(1)} %collective-permute-done.12.rest_1_, ...), custom_call_target="tpu_custom_call" | custom-call | bytes 1180172 | tf_op jit(solution)/shard_map/second_up/pallas_call | solution.py:34
  102.1 4.2 %all-to-all-done.2.both_ref = bf16[8,2,16,768]{3,2,1,0:T(8,128)(2,1)S(1)} async-done(((bf16[8,2,16,768]{3,2,1,0:T(8,128)(2,1)}), bf16[8,2,16,768]{3,2,1,0:T(8,128)(2,1)S(1)}, u32[]{:S(2)}, u32[]{:S(2)}) %all-to-all-start.2) | async-done | bytes 393248 | tf_op jit(solution)/shard_map/all_to_all | solution.py:267
  106.3 4.9 %all-to-all-start.1 = ((bf16[8,2,16,768]{3,2,1,0:T(8,128)(2,1)}), bf16[8,2,16,768]{3,2,1,0:T(8,128)(2,1)S(1)}, u32[]{:S(2)}, u32[]{:S(2)}) async-start(bf16[8,2,16,768]{3,2,1,0:T(8,128)(2,1)} %second_up.1), calls=%async_computation.1 | async-start | bytes 786432 | tf_op jit(solution)/shard_map/all_to_all | solution.py:267
  111.8 4.8 %collective-permute-start.22 = (bf16[8,16,768]{2,1,0:T(8,128)(2,1)S(1)}, bf16[8,16,768]{2,1,0:T(8,128)(2,1)S(1)}, u32[]{:S(2)}, u32[]{:S(2)}) collective-permute-start(bf16[8,16,768]{2,1,0:T(8,128)(2,1)S(1)} %get-tuple-element.64), channel_id=1, source_target_pairs={{0,4},{4,8},{8,12},{12,16},{16,20},{20,24},{24,28},{28,0},{1,5},{5... | collective-permute-start | bytes 589832 | tf_op jit(solution)/shard_map/ppermute | solution.py:252
  116.6 2.0 %collective-permute-start.24 = (bf16[8,16,768]{2,1,0:T(8,128)(2,1)S(1)}, bf16[8,16,768]{2,1,0:T(8,128)(2,1)S(1)}, u32[]{:S(2)}, u32[]{:S(2)}) collective-permute-start(bf16[8,16,768]{2,1,0:T(8,128)(2,1)S(1)} %get-tuple-element.66), channel_id=1, source_target_pairs={{0,24},{4,12},{8,0},{12,20},{16,8},{20,28},{24,16},{28,4},{1,25},{... | collective-permute-start | bytes 589832 | tf_op jit(solution)/shard_map/ppermute | solution.py:255
  119.2 4.7 %collective-permute-start.19 = (bf16[8,16,768]{2,1,0:T(8,128)(2,1)S(1)}, bf16[8,16,768]{2,1,0:T(8,128)(2,1)S(1)}, u32[]{:S(2)}, u32[]{:S(2)}) collective-permute-start(bf16[8,16,768]{2,1,0:T(8,128)(2,1)S(1)} %get-tuple-element.60), channel_id=1, source_target_pairs={{0,4},{4,8},{8,12},{12,16},{16,20},{20,24},{24,28},{28,0},{1,5},{5... | collective-permute-start | bytes 589832 | tf_op jit(solution)/shard_map/ppermute | solution.py:252
  123.9 2.0 %collective-permute-start.21 = (bf16[8,16,768]{2,1,0:T(8,128)(2,1)S(1)}, bf16[8,16,768]{2,1,0:T(8,128)(2,1)S(1)}, u32[]{:S(2)}, u32[]{:S(2)}) collective-permute-start(bf16[8,16,768]{2,1,0:T(8,128)(2,1)S(1)} %get-tuple-element.62), channel_id=1, source_target_pairs={{0,24},{4,12},{8,0},{12,20},{16,8},{20,28},{24,16},{28,4},{1,25},{... | collective-permute-start | bytes 589832 | tf_op jit(solution)/shard_map/ppermute | solution.py:255
  129.2 4.2 %collective-permute-done.19.before_ref = bf16[8,16,768]{2,1,0:T(8,128)(2,1)S(1)} collective-permute-done((bf16[8,16,768]{2,1,0:T(8,128)(2,1)S(1)}, bf16[8,16,768]{2,1,0:T(8,128)(2,1)S(1)}, u32[]{:S(2)}, u32[]{:S(2)}) %collective-permute-start.19) | collective-permute-done | bytes 196640 | tf_op jit(solution)/shard_map/ppermute | solution.py:252
  (62 shorter events, 29.7 us)
Async XLA Ops:
  2.7 3.5 %collective-permute-start = (bf16[64,1536]{1,0:T(8,128)(2,1)S(1)}, bf16[64,1536]{1,0:T(8,128)(2,1)S(1)}, u32[]{:S(2)}, u32[]{:S(2)}) collective-permute-start(bf16[64,1536]{1,0:T(8,128)(2,1)S(1)} %get-tuple-element.35), channel_id=1, source_target_pairs={{0,1},{1,0},{2,3},{3,2},{4,5},{5,4},{6,7},{7,6},{8,9},{9,8},{10,11... | collective-permute-start | bytes 589832 | tf_op jit(solution)/shard_map/ppermute | solution.py:191
  2.8 9.3 %collective-permute-start.4 = (bf16[64,1536]{1,0:T(8,128)(2,1)S(1)}, bf16[64,1536]{1,0:T(8,128)(2,1)S(1)}, u32[]{:S(2)}, u32[]{:S(2)}) collective-permute-start(bf16[64,1536]{1,0:T(8,128)(2,1)S(1)} %get-tuple-element.41), channel_id=1, source_target_pairs={{0,2},{1,3},{2,0},{3,1},{4,6},{5,7},{6,4},{7,5},{8,10},{9,11},{10,... | collective-permute-start | bytes 589832 | tf_op jit(solution)/shard_map/ppermute | solution.py:191
  4.1 11.2 %collective-permute-start.5 = (bf16[64,1536]{1,0:T(8,128)(2,1)S(1)}, bf16[64,1536]{1,0:T(8,128)(2,1)S(1)}, u32[]{:S(2)}, u32[]{:S(2)}) collective-permute-start(bf16[64,1536]{1,0:T(8,128)(2,1)S(1)} %get-tuple-element.42), channel_id=1, source_target_pairs={{0,3},{1,2},{2,1},{3,0},{4,7},{5,6},{6,5},{7,4},{8,11},{9,10},{10,... | collective-permute-start | bytes 589832 | tf_op jit(solution)/shard_map/ppermute | solution.py:191
  8.0 9.8 %collective-permute-start.1 = (bf16[64,1536]{1,0:T(8,128)(2,1)S(1)}, bf16[64,1536]{1,0:T(8,128)(2,1)S(1)}, u32[]{:S(2)}, u32[]{:S(2)}) collective-permute-start(bf16[64,1536]{1,0:T(8,128)(2,1)S(1)} %get-tuple-element.37), channel_id=1, source_target_pairs={{0,1},{1,0},{2,3},{3,2},{4,5},{5,4},{6,7},{7,6},{8,9},{9,8},{10,11... | collective-permute-start | bytes 589832 | tf_op jit(solution)/shard_map/ppermute | solution.py:191
  8.5 12.0 %collective-permute-start.2 = (bf16[64,1536]{1,0:T(8,128)(2,1)S(1)}, bf16[64,1536]{1,0:T(8,128)(2,1)S(1)}, u32[]{:S(2)}, u32[]{:S(2)}) collective-permute-start(bf16[64,1536]{1,0:T(8,128)(2,1)S(1)} %get-tuple-element.38), channel_id=1, source_target_pairs={{0,2},{1,3},{2,0},{3,1},{4,6},{5,7},{6,4},{7,5},{8,10},{9,11},{10,... | collective-permute-start | bytes 589832 | tf_op jit(solution)/shard_map/ppermute | solution.py:191
  9.7 14.1 %collective-permute-start.3 = (bf16[64,1536]{1,0:T(8,128)(2,1)S(1)}, bf16[64,1536]{1,0:T(8,128)(2,1)S(1)}, u32[]{:S(2)}, u32[]{:S(2)}) collective-permute-start(bf16[64,1536]{1,0:T(8,128)(2,1)S(1)} %get-tuple-element.39), channel_id=1, source_target_pairs={{0,3},{1,2},{2,1},{3,0},{4,7},{5,6},{6,5},{7,4},{8,11},{9,10},{10,... | collective-permute-start | bytes 589832 | tf_op jit(solution)/shard_map/ppermute | solution.py:191
  24.8 7.8 %collective-permute-start.9 = (bf16[128,512]{1,0:T(8,128)(2,1)S(1)}, bf16[128,512]{1,0:T(8,128)(2,1)S(1)}, u32[]{:S(2)}, u32[]{:S(2)}) collective-permute-start(bf16[128,512]{1,0:T(8,128)(2,1)S(1)} %pair_pre.1.rest_0_.both_ref), channel_id=1, source_target_pairs={{0,2},{1,3},{2,0},{3,1},{4,6},{5,7},{6,4},{7,5},{8,10},{9,11},{10,... | collective-permute-start | bytes 393224 | tf_op jit(solution)/shard_map/ppermute | solution.py:191
  26.0 8.7 %collective-permute-start.8 = (bf16[128,512]{1,0:T(8,128)(2,1)S(1)}, bf16[128,512]{1,0:T(8,128)(2,1)S(1)}, u32[]{:S(2)}, u32[]{:S(2)}) collective-permute-start(bf16[128,512]{1,0:T(8,128)(2,1)S(1)} %pair_hid.1.both_ref), channel_id=1, source_target_pairs={{0,2},{1,3},{2,0},{3,1},{4,6},{5,7},{6,4},{7,5},{8,10},{9,11},{10,... | collective-permute-start | bytes 393224 | tf_op jit(solution)/shard_map/ppermute | solution.py:191
  32.8 2.1 %collective-permute-start.11 = (bf16[128,512]{1,0:T(8,128)(2,1)S(1)}, bf16[128,512]{1,0:T(8,128)(2,1)S(1)}, u32[]{:S(2)}, u32[]{:S(2)}) collective-permute-start(bf16[128,512]{1,0:T(8,128)(2,1)S(1)} %get-tuple-element.49.own_ref), channel_id=1, source_target_pairs={{0,1},{1,0},{2,3},{3,2},{4,5},{5,4},{6,7},{7,6},{8,9},{9,8},{10,11... | collective-permute-start | bytes 393224 | tf_op jit(solution)/shard_map/ppermute | solution.py:191
  68.4 10.8 %collective-permute-start.12 = (bf16[2,2,16,768]{3,2,1,0:T(8,128)(2,1)S(1)}, bf16[2,2,16,768]{3,2,1,0:T(8,128)(2,1)S(1)}, u32[]{:S(2)}, u32[]{:S(2)}) collective-permute-start(bf16[2,2,16,768]{3,2,1,0:T(8,128)(2,1)S(1)} %get-tuple-element.52), channel_id=1, source_target_pairs={{0,4},{4,8},{8,12},{12,16},{16,20},{20,24},{24,28},{28,0},{1,5},{5... | collective-permute-start | bytes 294920 | tf_op jit(solution)/shard_map/ppermute | solution.py:252
  70.3 13.2 %collective-permute-start.13 = (bf16[2,2,16,768]{3,2,1,0:T(8,128)(2,1)S(1)}, bf16[2,2,16,768]{3,2,1,0:T(8,128)(2,1)S(1)}, u32[]{:S(2)}, u32[]{:S(2)}) collective-permute-start(bf16[2,2,16,768]{3,2,1,0:T(8,128)(2,1)S(1)} %get-tuple-element.53), channel_id=1, source_target_pairs={{0,28},{4,0},{8,4},{12,8},{16,12},{20,16},{24,20},{28,24},{1,29},{... | collective-permute-start | bytes 294920 | tf_op jit(solution)/shard_map/ppermute | solution.py:252
  74.4 13.7 %collective-permute-start.14 = (bf16[2,2,16,768]{3,2,1,0:T(8,128)(2,1)S(1)}, bf16[2,2,16,768]{3,2,1,0:T(8,128)(2,1)S(1)}, u32[]{:S(2)}, u32[]{:S(2)}) collective-permute-start(bf16[2,2,16,768]{3,2,1,0:T(8,128)(2,1)S(1)} %get-tuple-element.54), channel_id=1, source_target_pairs={{0,8},{4,12},{8,16},{12,20},{16,24},{20,28},{24,0},{28,4},{1,9},{5... | collective-permute-start | bytes 294920 | tf_op jit(solution)/shard_map/ppermute | solution.py:252
  74.4 13.7 %collective-permute-start.15 = (bf16[2,2,16,768]{3,2,1,0:T(8,128)(2,1)S(1)}, bf16[2,2,16,768]{3,2,1,0:T(8,128)(2,1)S(1)}, u32[]{:S(2)}, u32[]{:S(2)}) collective-permute-start(bf16[2,2,16,768]{3,2,1,0:T(8,128)(2,1)S(1)} %get-tuple-element.55), channel_id=1, source_target_pairs={{0,24},{4,28},{8,0},{12,4},{16,8},{20,12},{24,16},{28,20},{1,25},{... | collective-permute-start | bytes 294920 | tf_op jit(solution)/shard_map/ppermute | solution.py:252
  78.5 12.2 %collective-permute-start.16 = (bf16[2,2,16,768]{3,2,1,0:T(8,128)(2,1)S(1)}, bf16[2,2,16,768]{3,2,1,0:T(8,128)(2,1)S(1)}, u32[]{:S(2)}, u32[]{:S(2)}) collective-permute-start(bf16[2,2,16,768]{3,2,1,0:T(8,128)(2,1)S(1)} %get-tuple-element.56), channel_id=1, source_target_pairs={{0,12},{4,16},{8,20},{12,24},{16,28},{20,0},{24,4},{28,8},{1,13},{... | collective-permute-start | bytes 294920 | tf_op jit(solution)/shard_map/ppermute | solution.py:252
  79.1 14.4 %collective-permute-start.17 = (bf16[2,2,16,768]{3,2,1,0:T(8,128)(2,1)S(1)}, bf16[2,2,16,768]{3,2,1,0:T(8,128)(2,1)S(1)}, u32[]{:S(2)}, u32[]{:S(2)}) collective-permute-start(bf16[2,2,16,768]{3,2,1,0:T(8,128)(2,1)S(1)} %get-tuple-element.57), channel_id=1, source_target_pairs={{0,20},{4,24},{8,28},{12,0},{16,4},{20,8},{24,12},{28,16},{1,21},{... | collective-permute-start | bytes 294920 | tf_op jit(solution)/shard_map/ppermute | solution.py:252
  83.6 10.1 %collective-permute-start.18 = (bf16[2,2,16,768]{3,2,1,0:T(8,128)(2,1)S(1)}, bf16[2,2,16,768]{3,2,1,0:T(8,128)(2,1)S(1)}, u32[]{:S(2)}, u32[]{:S(2)}) collective-permute-start(bf16[2,2,16,768]{3,2,1,0:T(8,128)(2,1)S(1)} %get-tuple-element.58), channel_id=1, source_target_pairs={{0,16},{4,20},{8,24},{12,28},{16,0},{20,4},{24,8},{28,12},{1,17},{... | collective-permute-start | bytes 294920 | tf_op jit(solution)/shard_map/ppermute | solution.py:252
  96.0 10.3 %all-to-all-start.2 = ((bf16[8,2,16,768]{3,2,1,0:T(8,128)(2,1)}), bf16[8,2,16,768]{3,2,1,0:T(8,128)(2,1)S(1)}, u32[]{:S(2)}, u32[]{:S(2)}) async-start(bf16[8,2,16,768]{3,2,1,0:T(8,128)(2,1)} %second_down.1), calls=%async_computation.2 | async-start | bytes 786432 | tf_op jit(solution)/shard_map/all_to_all | solution.py:267
  106.3 12.3 %all-to-all-start.1 = ((bf16[8,2,16,768]{3,2,1,0:T(8,128)(2,1)}), bf16[8,2,16,768]{3,2,1,0:T(8,128)(2,1)S(1)}, u32[]{:S(2)}, u32[]{:S(2)}) async-start(bf16[8,2,16,768]{3,2,1,0:T(8,128)(2,1)} %second_up.1), calls=%async_computation.1 | async-start | bytes 786432 | tf_op jit(solution)/shard_map/all_to_all | solution.py:267
  111.8 12.1 %collective-permute-start.22 = (bf16[8,16,768]{2,1,0:T(8,128)(2,1)S(1)}, bf16[8,16,768]{2,1,0:T(8,128)(2,1)S(1)}, u32[]{:S(2)}, u32[]{:S(2)}) collective-permute-start(bf16[8,16,768]{2,1,0:T(8,128)(2,1)S(1)} %get-tuple-element.64), channel_id=1, source_target_pairs={{0,4},{4,8},{8,12},{12,16},{16,20},{20,24},{24,28},{28,0},{1,5},{5... | collective-permute-start | bytes 589832 | tf_op jit(solution)/shard_map/ppermute | solution.py:252
  116.6 11.1 %collective-permute-start.23 = (bf16[8,16,768]{2,1,0:T(8,128)(2,1)S(1)}, bf16[8,16,768]{2,1,0:T(8,128)(2,1)S(1)}, u32[]{:S(2)}, u32[]{:S(2)}) collective-permute-start(bf16[8,16,768]{2,1,0:T(8,128)(2,1)S(1)} %get-tuple-element.65), channel_id=1, source_target_pairs={{0,28},{4,0},{8,4},{12,8},{16,12},{20,16},{24,20},{28,24},{1,29},{... | collective-permute-start | bytes 589832 | tf_op jit(solution)/shard_map/ppermute | solution.py:252
  116.6 11.1 %collective-permute-start.24 = (bf16[8,16,768]{2,1,0:T(8,128)(2,1)S(1)}, bf16[8,16,768]{2,1,0:T(8,128)(2,1)S(1)}, u32[]{:S(2)}, u32[]{:S(2)}) collective-permute-start(bf16[8,16,768]{2,1,0:T(8,128)(2,1)S(1)} %get-tuple-element.66), channel_id=1, source_target_pairs={{0,24},{4,12},{8,0},{12,20},{16,8},{20,28},{24,16},{28,4},{1,25},{... | collective-permute-start | bytes 589832 | tf_op jit(solution)/shard_map/ppermute | solution.py:255
  119.2 14.1 %collective-permute-start.19 = (bf16[8,16,768]{2,1,0:T(8,128)(2,1)S(1)}, bf16[8,16,768]{2,1,0:T(8,128)(2,1)S(1)}, u32[]{:S(2)}, u32[]{:S(2)}) collective-permute-start(bf16[8,16,768]{2,1,0:T(8,128)(2,1)S(1)} %get-tuple-element.60), channel_id=1, source_target_pairs={{0,4},{4,8},{8,12},{12,16},{16,20},{20,24},{24,28},{28,0},{1,5},{5... | collective-permute-start | bytes 589832 | tf_op jit(solution)/shard_map/ppermute | solution.py:252
  123.9 11.2 %collective-permute-start.20 = (bf16[8,16,768]{2,1,0:T(8,128)(2,1)S(1)}, bf16[8,16,768]{2,1,0:T(8,128)(2,1)S(1)}, u32[]{:S(2)}, u32[]{:S(2)}) collective-permute-start(bf16[8,16,768]{2,1,0:T(8,128)(2,1)S(1)} %get-tuple-element.61), channel_id=1, source_target_pairs={{0,28},{4,0},{8,4},{12,8},{16,12},{20,16},{24,20},{28,24},{1,29},{... | collective-permute-start | bytes 589832 | tf_op jit(solution)/shard_map/ppermute | solution.py:252
  123.9 11.2 %collective-permute-start.21 = (bf16[8,16,768]{2,1,0:T(8,128)(2,1)S(1)}, bf16[8,16,768]{2,1,0:T(8,128)(2,1)S(1)}, u32[]{:S(2)}, u32[]{:S(2)}) collective-permute-start(bf16[8,16,768]{2,1,0:T(8,128)(2,1)S(1)} %get-tuple-element.62), channel_id=1, source_target_pairs={{0,24},{4,12},{8,0},{12,20},{16,8},{20,28},{24,16},{28,4},{1,25},{... | collective-permute-start | bytes 589832 | tf_op jit(solution)/shard_map/ppermute | solution.py:255
  (9 other events, 93.4 us)

commit v5 on v4

--- a/solution.py
+++ b/solution.py
@@ -176,7 +176,7 @@
             out[c] = both_ref[c, label]
 
 
-def last_body(n_rx, pos_ref, own_ref, before_ref, after_ref, far_ref, out_ref):
+def last_body(n_rx, pos_ref, own_ref, far_ref, before_ref, after_ref, out_ref):
     k = pos_ref[2]
     width = own_ref.shape[2]
     for q, ref in ((0, own_ref), (TP - 1, before_ref), (1, after_ref), (2, far_ref)):
@@ -268,7 +268,7 @@
         own, after, before, far = call(
             functools.partial(pick_body, n_rx, n_ry), [shape((n_rx, SLAB, feat // 2))] * 4, [pos, group_y, news], "ssv", name="pick_" + name
         )
-        held = [own, along(after, 1), along(before, -1), two_away(far)]
+        held = [own, two_away(far), along(after, 1), along(before, -1)]
         (out,) = call(functools.partial(last_body, n_rx), [shape((rows, width))], [pos, *held], "svvvv", name="last_" + name)
         return out
 

time: 137 us -> 138 us (level)
    ppermute x2, starting transfers between devices: 3.93 us -> 8.15 us  [two_away(): lax.ppermute(value, 'ry', [(k, (k + (2 if k % 2 else n_ry - 2)) % n_ry) f...]
    ppermute x11, starting transfers between devices: 29.2 us -> 26.2 us  [along(): lax.ppermute(value, 'ry', [(k, (k + shift) % n_ry) for k in range(n_ry)])]
  transfers between devices with their start and end apart: 27 -> 27, of which waited for: 13 -> 12; matrix products, arithmetic and copies ran while one was open for 0% -> 0% of each run, Pallas kernels for 8% -> 7%
where the time goes in v5:
time: 138 us
  starting transfers between devices  54.9 us (40%)
  waiting for transfers between devices  32.3 us (23%)
  blocking collectives  28.7 us (21%)
  Pallas kernels  18.4 us (13%)
  local copies, waits for them, and re-layouts  2.39 us (2%)
    all_to_all x1, blocking collectives, shards(): lax.all_to_all(steps.reshape(n_rx * TP, 2, SLAB, feat // 2), ('rx', 'tp')...  28.7 us
    ppermute x11, starting transfers between devices, along(): lax.ppermute(value, 'ry', [(k, (k + shift) % n_ry) for k in range(n_ry)])  26.2 us
    pallas_call x18, Pallas kernels, call(): pl.pallas_call(body, out_shape=list(outs), in_specs=[kinds[c] for c in sp...  18.4 us
    ppermute x12, waiting for transfers between devices, swap(): return lax.ppermute(value, 'tp', [(t, t ^ r) for t in range(TP)])  16.8 us
    ppermute x12, starting transfers between devices, swap(): return lax.ppermute(value, 'tp', [(t, t ^ r) for t in range(TP)])  12 us
    ppermute x11, waiting for transfers between devices, along(): lax.ppermute(value, 'ry', [(k, (k + shift) % n_ry) for k in range(n_ry)])  11.4 us
    all_to_all x2, starting transfers between devices, averaged(): news = lax.all_to_all(news, 'rx', 0, 0, tiled=True)  8.67 us
    ppermute x2, starting transfers between devices, two_away(): lax.ppermute(value, 'ry', [(k, (k + (2 if k % 2 else n_ry - 2)) % n_ry) f...  8.15 us
  transfers between devices with their start and end apart: 27, of which 12 were waited for; matrix products, arithmetic and copies ran while one was open for 0% of the time, Pallas kernels for 7%

profile of v5, /device:TPU:24, one launch (start us, length us, event | category | flops | bytes accessed | tf_op | source)
XLA Modules:
  0.0 137.7 jit_solution(4344558012881880148)
XLA Ops:
  4.1 2.0 %collective-permute-start.5 = (bf16[64,1536]{1,0:T(8,128)(2,1)S(1)}, bf16[64,1536]{1,0:T(8,128)(2,1)S(1)}, u32[]{:S(2)}, u32[]{:S(2)}) collective-permute-start(bf16[64,1536]{1,0:T(8,128)(2,1)S(1)} %get-tuple-element.42), channel_id=1, source_target_pairs={{0,3},{1,2},{2,1},{3,0},{4,7},{5,6},{6,5},{7,4},{8,11},{9,10},{10,... | collective-permute-start | bytes 589832 | tf_op jit(solution)/shard_map/ppermute | solution.py:191
  12.1 3.3 %collective-permute-done.5.w3 = bf16[64,1536]{1,0:T(8,128)(2,1)S(1)} collective-permute-done((bf16[64,1536]{1,0:T(8,128)(2,1)S(1)}, bf16[64,1536]{1,0:T(8,128)(2,1)S(1)}, u32[]{:S(2)}, u32[]{:S(2)}) %collective-permute-start.5) | collective-permute-done | bytes 196640 | tf_op jit(solution)/shard_map/ppermute | solution.py:191
  17.9 2.7 %collective-permute-done.2.w2 = bf16[64,1536]{1,0:T(8,128)(2,1)S(1)} collective-permute-done((bf16[64,1536]{1,0:T(8,128)(2,1)S(1)}, bf16[64,1536]{1,0:T(8,128)(2,1)S(1)}, u32[]{:S(2)}, u32[]{:S(2)}) %collective-permute-start.2) | collective-permute-done | bytes 196640 | tf_op jit(solution)/shard_map/ppermute | solution.py:191
  20.5 3.3 %collective-permute-done.3.w3 = bf16[64,1536]{1,0:T(8,128)(2,1)S(1)} collective-permute-done((bf16[64,1536]{1,0:T(8,128)(2,1)S(1)}, bf16[64,1536]{1,0:T(8,128)(2,1)S(1)}, u32[]{:S(2)}, u32[]{:S(2)}) %collective-permute-start.3) | collective-permute-done | bytes 196640 | tf_op jit(solution)/shard_map/ppermute | solution.py:191
  26.0 2.4 %collective-permute-start.8 = (bf16[128,512]{1,0:T(8,128)(2,1)S(1)}, bf16[128,512]{1,0:T(8,128)(2,1)S(1)}, u32[]{:S(2)}, u32[]{:S(2)}) collective-permute-start(bf16[128,512]{1,0:T(8,128)(2,1)S(1)} %pair_hid.1.both_ref), channel_id=1, source_target_pairs={{0,2},{1,3},{2,0},{3,1},{4,6},{5,7},{6,4},{7,5},{8,10},{9,11},{10,... | collective-permute-start | bytes 393224 | tf_op jit(solution)/shard_map/ppermute | solution.py:191
  28.4 4.2 %collective-permute-done.9.far_ref = bf16[128,512]{1,0:T(8,128)(2,1)S(1)} collective-permute-done((bf16[128,512]{1,0:T(8,128)(2,1)S(1)}, bf16[128,512]{1,0:T(8,128)(2,1)S(1)}, u32[]{:S(2)}, u32[]{:S(2)}) %collective-permute-start.9) | collective-permute-done | bytes 131104 | tf_op jit(solution)/shard_map/ppermute | solution.py:191
  38.5 28.7 %all_to_all.15.terms_ref = bf16[32,2,16,768]{3,2,1,0:T(8,128)(2,1)S(1)} all-to-all(bf16[32,2,16,768]{3,2,1,0:T(8,128)(2,1)S(1)} %bitcast.11), channel_id=1, replica_groups=mesh['rx'=8,'ry'=8,'tp'=4] {'rx','tp'}, dimensions={0} | all-to-all | bytes 3145728 | tf_op jit(solution)/shard_map/all_to_all | solution.py:250
  68.4 2.0 %collective-permute-start.12 = (bf16[2,2,16,768]{3,2,1,0:T(8,128)(2,1)S(1)}, bf16[2,2,16,768]{3,2,1,0:T(8,128)(2,1)S(1)}, u32[]{:S(2)}, u32[]{:S(2)}) collective-permute-start(bf16[2,2,16,768]{3,2,1,0:T(8,128)(2,1)S(1)} %get-tuple-element.52), channel_id=1, source_target_pairs={{0,4},{4,8},{8,12},{12,16},{16,20},{20,24},{24,28},{28,0},{1,5},{5... | collective-permute-start | bytes 294920 | tf_op jit(solution)/shard_map/ppermute | solution.py:252
  70.3 4.0 %collective-permute-start.13 = (bf16[2,2,16,768]{3,2,1,0:T(8,128)(2,1)S(1)}, bf16[2,2,16,768]{3,2,1,0:T(8,128)(2,1)S(1)}, u32[]{:S(2)}, u32[]{:S(2)}) collective-permute-start(bf16[2,2,16,768]{3,2,1,0:T(8,128)(2,1)S(1)} %get-tuple-element.53), channel_id=1, source_target_pairs={{0,28},{4,0},{8,4},{12,8},{16,12},{20,16},{24,20},{28,24},{1,29},{... | collective-permute-start | bytes 294920 | tf_op jit(solution)/shard_map/ppermute | solution.py:252
  74.4 4.1 %collective-permute-start.15 = (bf16[2,2,16,768]{3,2,1,0:T(8,128)(2,1)S(1)}, bf16[2,2,16,768]{3,2,1,0:T(8,128)(2,1)S(1)}, u32[]{:S(2)}, u32[]{:S(2)}) collective-permute-start(bf16[2,2,16,768]{3,2,1,0:T(8,128)(2,1)S(1)} %get-tuple-element.55), channel_id=1, source_target_pairs={{0,24},{4,28},{8,0},{12,4},{16,8},{20,12},{24,16},{28,20},{1,25},{... | collective-permute-start | bytes 294920 | tf_op jit(solution)/shard_map/ppermute | solution.py:252
  79.1 4.4 %collective-permute-start.17 = (bf16[2,2,16,768]{3,2,1,0:T(8,128)(2,1)S(1)}, bf16[2,2,16,768]{3,2,1,0:T(8,128)(2,1)S(1)}, u32[]{:S(2)}, u32[]{:S(2)}) collective-permute-start(bf16[2,2,16,768]{3,2,1,0:T(8,128)(2,1)S(1)} %get-tuple-element.57), channel_id=1, source_target_pairs={{0,20},{4,24},{8,28},{12,0},{16,4},{20,8},{24,12},{28,16},{1,21},{... | collective-permute-start | bytes 294920 | tf_op jit(solution)/shard_map/ppermute | solution.py:252
  83.6 4.5 %collective-permute-start.18 = (bf16[2,2,16,768]{3,2,1,0:T(8,128)(2,1)S(1)}, bf16[2,2,16,768]{3,2,1,0:T(8,128)(2,1)S(1)}, u32[]{:S(2)}, u32[]{:S(2)}) collective-permute-start(bf16[2,2,16,768]{3,2,1,0:T(8,128)(2,1)S(1)} %get-tuple-element.58), channel_id=1, source_target_pairs={{0,16},{4,20},{8,24},{12,28},{16,0},{20,4},{24,8},{28,12},{1,17},{... | collective-permute-start | bytes 294920 | tf_op jit(solution)/shard_map/ppermute | solution.py:252
  88.0 2.6 %collective-permute-done.16.rest_5_ = bf16[2,2,16,768]{3,2,1,0:T(8,128)(2,1)S(1)} collective-permute-done((bf16[2,2,16,768]{3,2,1,0:T(8,128)(2,1)S(1)}, bf16[2,2,16,768]{3,2,1,0:T(8,128)(2,1)S(1)}, u32[]{:S(2)}, u32[]{:S(2)}) %collective-permute-start.16) | collective-permute-done | bytes 98336 | tf_op jit(solution)/shard_map/ppermute | solution.py:252
  90.7 2.8 %collective-permute-done.17.rest_6_ = bf16[2,2,16,768]{3,2,1,0:T(8,128)(2,1)S(1)} collective-permute-done((bf16[2,2,16,768]{3,2,1,0:T(8,128)(2,1)S(1)}, bf16[2,2,16,768]{3,2,1,0:T(8,128)(2,1)S(1)}, u32[]{:S(2)}, u32[]{:S(2)}) %collective-permute-start.17) | collective-permute-done | bytes 98336 | tf_op jit(solution)/shard_map/ppermute | solution.py:252
  93.6 2.3 %second_down.1 = bf16[8,2,16,768]{3,2,1,0:T(8,128)(2,1)} custom-call(s32[3]{0:T(128)S(1)} %pad_add_fusion.pos_ref, s32[8,8]{1,0:T(8,128)S(1)} %copy-done.5, s32[8,8]{1,0:T(8,128)S(1)} %copy-done.4, bf16[2,2,16,768]{3,2,1,0:T(8,128)(2,1)S(1)} %get-tuple-element.51.rest_0_, bf16[2,2,16,768]{3,2,1,0:T(8,128)(2,1)S(1)} %collective-permute-done.12.rest_1_, ...), custom_call_target="tpu_custom_call" | custom-call | bytes 1180172 | tf_op jit(solution)/shard_map/second_down/pallas_call | solution.py:34
  96.0 3.8 %all-to-all-start.2 = ((bf16[8,2,16,768]{3,2,1,0:T(8,128)(2,1)}), bf16[8,2,16,768]{3,2,1,0:T(8,128)(2,1)S(1)}, u32[]{:S(2)}, u32[]{:S(2)}) async-start(bf16[8,2,16,768]{3,2,1,0:T(8,128)(2,1)} %second_down.1), calls=%async_computation.2 | async-start | bytes 786432 | tf_op jit(solution)/shard_map/all_to_all | solution.py:267
  99.8 2.3 %second_up.1 = bf16[8,2,16,768]{3,2,1,0:T(8,128)(2,1)} custom-call(s32[3]{0:T(128)S(1)} %pad_add_fusion.pos_ref, s32[8,8]{1,0:T(8,128)S(1)} %copy-done.5, s32[8,8]{1,0:T(8,128)S(1)} %copy-done.4, bf16[2,2,16,768]{3,2,1,0:T(8,128)(2,1)S(1)} %get-tuple-element.51.rest_0_, bf16[2,2,16,768]{3,2,1,0:T(8,128)(2,1)S(1)} %collective-permute-done.12.rest_1_, ...), custom_call_target="tpu_custom_call" | custom-call | bytes 1180172 | tf_op jit(solution)/shard_map/second_up/pallas_call | solution.py:34
  102.1 4.2 %all-to-all-done.2.both_ref = bf16[8,2,16,768]{3,2,1,0:T(8,128)(2,1)S(1)} async-done(((bf16[8,2,16,768]{3,2,1,0:T(8,128)(2,1)}), bf16[8,2,16,768]{3,2,1,0:T(8,128)(2,1)S(1)}, u32[]{:S(2)}, u32[]{:S(2)}) %all-to-all-start.2) | async-done | bytes 393248 | tf_op jit(solution)/shard_map/all_to_all | solution.py:267
  106.3 4.9 %all-to-all-start.1 = ((bf16[8,2,16,768]{3,2,1,0:T(8,128)(2,1)}), bf16[8,2,16,768]{3,2,1,0:T(8,128)(2,1)S(1)}, u32[]{:S(2)}, u32[]{:S(2)}) async-start(bf16[8,2,16,768]{3,2,1,0:T(8,128)(2,1)} %second_up.1), calls=%async_computation.1 | async-start | bytes 786432 | tf_op jit(solution)/shard_map/all_to_all | solution.py:267
  111.8 4.7 %collective-permute-start.22 = (bf16[8,16,768]{2,1,0:T(8,128)(2,1)S(1)}, bf16[8,16,768]{2,1,0:T(8,128)(2,1)S(1)}, u32[]{:S(2)}, u32[]{:S(2)}) collective-permute-start(bf16[8,16,768]{2,1,0:T(8,128)(2,1)S(1)} %get-tuple-element.64), channel_id=1, source_target_pairs={{0,24},{4,12},{8,0},{12,20},{16,8},{20,28},{24,16},{28,4},{1,25},{... | collective-permute-start | bytes 589832 | tf_op jit(solution)/shard_map/ppermute | solution.py:255
  116.7 3.1 %collective-permute-start.24 = (bf16[8,16,768]{2,1,0:T(8,128)(2,1)S(1)}, bf16[8,16,768]{2,1,0:T(8,128)(2,1)S(1)}, u32[]{:S(2)}, u32[]{:S(2)}) collective-permute-start(bf16[8,16,768]{2,1,0:T(8,128)(2,1)S(1)} %get-tuple-element.66), channel_id=1, source_target_pairs={{0,28},{4,0},{8,4},{12,8},{16,12},{20,16},{24,20},{28,24},{1,29},{... | collective-permute-start | bytes 589832 | tf_op jit(solution)/shard_map/ppermute | solution.py:252
  120.4 3.4 %collective-permute-start.19 = (bf16[8,16,768]{2,1,0:T(8,128)(2,1)S(1)}, bf16[8,16,768]{2,1,0:T(8,128)(2,1)S(1)}, u32[]{:S(2)}, u32[]{:S(2)}) collective-permute-start(bf16[8,16,768]{2,1,0:T(8,128)(2,1)S(1)} %get-tuple-element.60), channel_id=1, source_target_pairs={{0,24},{4,12},{8,0},{12,20},{16,8},{20,28},{24,16},{28,4},{1,25},{... | collective-permute-start | bytes 589832 | tf_op jit(solution)/shard_map/ppermute | solution.py:255
  124.0 3.1 %collective-permute-start.21 = (bf16[8,16,768]{2,1,0:T(8,128)(2,1)S(1)}, bf16[8,16,768]{2,1,0:T(8,128)(2,1)S(1)}, u32[]{:S(2)}, u32[]{:S(2)}) collective-permute-start(bf16[8,16,768]{2,1,0:T(8,128)(2,1)S(1)} %get-tuple-element.62), channel_id=1, source_target_pairs={{0,28},{4,0},{8,4},{12,8},{16,12},{20,16},{24,20},{28,24},{1,29},{... | collective-permute-start | bytes 589832 | tf_op jit(solution)/shard_map/ppermute | solution.py:252
  130.4 5.8 %collective-permute-done.20.before_ref = bf16[8,16,768]{2,1,0:T(8,128)(2,1)S(1)} collective-permute-done((bf16[8,16,768]{2,1,0:T(8,128)(2,1)S(1)}, bf16[8,16,768]{2,1,0:T(8,128)(2,1)S(1)}, u32[]{:S(2)}, u32[]{:S(2)}) %collective-permute-start.20) | collective-permute-done | bytes 196640 | tf_op jit(solution)/shard_map/ppermute | solution.py:252
  (62 shorter events, 28.2 us)
Async XLA Ops:
  2.7 3.5 %collective-permute-start = (bf16[64,1536]{1,0:T(8,128)(2,1)S(1)}, bf16[64,1536]{1,0:T(8,128)(2,1)S(1)}, u32[]{:S(2)}, u32[]{:S(2)}) collective-permute-start(bf16[64,1536]{1,0:T(8,128)(2,1)S(1)} %get-tuple-element.35), channel_id=1, source_target_pairs={{0,1},{1,0},{2,3},{3,2},{4,5},{5,4},{6,7},{7,6},{8,9},{9,8},{10,11... | collective-permute-start | bytes 589832 | tf_op jit(solution)/shard_map/ppermute | solution.py:191
  2.8 9.3 %collective-permute-start.4 = (bf16[64,1536]{1,0:T(8,128)(2,1)S(1)}, bf16[64,1536]{1,0:T(8,128)(2,1)S(1)}, u32[]{:S(2)}, u32[]{:S(2)}) collective-permute-start(bf16[64,1536]{1,0:T(8,128)(2,1)S(1)} %get-tuple-element.41), channel_id=1, source_target_pairs={{0,2},{1,3},{2,0},{3,1},{4,6},{5,7},{6,4},{7,5},{8,10},{9,11},{10,... | collective-permute-start | bytes 589832 | tf_op jit(solution)/shard_map/ppermute | solution.py:191
  4.1 11.2 %collective-permute-start.5 = (bf16[64,1536]{1,0:T(8,128)(2,1)S(1)}, bf16[64,1536]{1,0:T(8,128)(2,1)S(1)}, u32[]{:S(2)}, u32[]{:S(2)}) collective-permute-start(bf16[64,1536]{1,0:T(8,128)(2,1)S(1)} %get-tuple-element.42), channel_id=1, source_target_pairs={{0,3},{1,2},{2,1},{3,0},{4,7},{5,6},{6,5},{7,4},{8,11},{9,10},{10,... | collective-permute-start | bytes 589832 | tf_op jit(solution)/shard_map/ppermute | solution.py:191
  8.0 9.8 %collective-permute-start.1 = (bf16[64,1536]{1,0:T(8,128)(2,1)S(1)}, bf16[64,1536]{1,0:T(8,128)(2,1)S(1)}, u32[]{:S(2)}, u32[]{:S(2)}) collective-permute-start(bf16[64,1536]{1,0:T(8,128)(2,1)S(1)} %get-tuple-element.37), channel_id=1, source_target_pairs={{0,1},{1,0},{2,3},{3,2},{4,5},{5,4},{6,7},{7,6},{8,9},{9,8},{10,11... | collective-permute-start | bytes 589832 | tf_op jit(solution)/shard_map/ppermute | solution.py:191
  8.5 12.0 %collective-permute-start.2 = (bf16[64,1536]{1,0:T(8,128)(2,1)S(1)}, bf16[64,1536]{1,0:T(8,128)(2,1)S(1)}, u32[]{:S(2)}, u32[]{:S(2)}) collective-permute-start(bf16[64,1536]{1,0:T(8,128)(2,1)S(1)} %get-tuple-element.38), channel_id=1, source_target_pairs={{0,2},{1,3},{2,0},{3,1},{4,6},{5,7},{6,4},{7,5},{8,10},{9,11},{10,... | collective-permute-start | bytes 589832 | tf_op jit(solution)/shard_map/ppermute | solution.py:191
  9.7 14.1 %collective-permute-start.3 = (bf16[64,1536]{1,0:T(8,128)(2,1)S(1)}, bf16[64,1536]{1,0:T(8,128)(2,1)S(1)}, u32[]{:S(2)}, u32[]{:S(2)}) collective-permute-start(bf16[64,1536]{1,0:T(8,128)(2,1)S(1)} %get-tuple-element.39), channel_id=1, source_target_pairs={{0,3},{1,2},{2,1},{3,0},{4,7},{5,6},{6,5},{7,4},{8,11},{9,10},{10,... | collective-permute-start | bytes 589832 | tf_op jit(solution)/shard_map/ppermute | solution.py:191
  24.8 7.8 %collective-permute-start.9 = (bf16[128,512]{1,0:T(8,128)(2,1)S(1)}, bf16[128,512]{1,0:T(8,128)(2,1)S(1)}, u32[]{:S(2)}, u32[]{:S(2)}) collective-permute-start(bf16[128,512]{1,0:T(8,128)(2,1)S(1)} %pair_pre.1.rest_0_.both_ref), channel_id=1, source_target_pairs={{0,2},{1,3},{2,0},{3,1},{4,6},{5,7},{6,4},{7,5},{8,10},{9,11},{10,... | collective-permute-start | bytes 393224 | tf_op jit(solution)/shard_map/ppermute | solution.py:191
  26.0 8.7 %collective-permute-start.8 = (bf16[128,512]{1,0:T(8,128)(2,1)S(1)}, bf16[128,512]{1,0:T(8,128)(2,1)S(1)}, u32[]{:S(2)}, u32[]{:S(2)}) collective-permute-start(bf16[128,512]{1,0:T(8,128)(2,1)S(1)} %pair_hid.1.both_ref), channel_id=1, source_target_pairs={{0,2},{1,3},{2,0},{3,1},{4,6},{5,7},{6,4},{7,5},{8,10},{9,11},{10,... | collective-permute-start | bytes 393224 | tf_op jit(solution)/shard_map/ppermute | solution.py:191
  32.8 2.1 %collective-permute-start.11 = (bf16[128,512]{1,0:T(8,128)(2,1)S(1)}, bf16[128,512]{1,0:T(8,128)(2,1)S(1)}, u32[]{:S(2)}, u32[]{:S(2)}) collective-permute-start(bf16[128,512]{1,0:T(8,128)(2,1)S(1)} %get-tuple-element.49.own_ref), channel_id=1, source_target_pairs={{0,1},{1,0},{2,3},{3,2},{4,5},{5,4},{6,7},{7,6},{8,9},{9,8},{10,11... | collective-permute-start | bytes 393224 | tf_op jit(solution)/shard_map/ppermute | solution.py:191
  68.4 10.8 %collective-permute-start.12 = (bf16[2,2,16,768]{3,2,1,0:T(8,128)(2,1)S(1)}, bf16[2,2,16,768]{3,2,1,0:T(8,128)(2,1)S(1)}, u32[]{:S(2)}, u32[]{:S(2)}) collective-permute-start(bf16[2,2,16,768]{3,2,1,0:T(8,128)(2,1)S(1)} %get-tuple-element.52), channel_id=1, source_target_pairs={{0,4},{4,8},{8,12},{12,16},{16,20},{20,24},{24,28},{28,0},{1,5},{5... | collective-permute-start | bytes 294920 | tf_op jit(solution)/shard_map/ppermute | solution.py:252
  70.3 13.2 %collective-permute-start.13 = (bf16[2,2,16,768]{3,2,1,0:T(8,128)(2,1)S(1)}, bf16[2,2,16,768]{3,2,1,0:T(8,128)(2,1)S(1)}, u32[]{:S(2)}, u32[]{:S(2)}) collective-permute-start(bf16[2,2,16,768]{3,2,1,0:T(8,128)(2,1)S(1)} %get-tuple-element.53), channel_id=1, source_target_pairs={{0,28},{4,0},{8,4},{12,8},{16,12},{20,16},{24,20},{28,24},{1,29},{... | collective-permute-start | bytes 294920 | tf_op jit(solution)/shard_map/ppermute | solution.py:252
  74.4 13.7 %collective-permute-start.14 = (bf16[2,2,16,768]{3,2,1,0:T(8,128)(2,1)S(1)}, bf16[2,2,16,768]{3,2,1,0:T(8,128)(2,1)S(1)}, u32[]{:S(2)}, u32[]{:S(2)}) collective-permute-start(bf16[2,2,16,768]{3,2,1,0:T(8,128)(2,1)S(1)} %get-tuple-element.54), channel_id=1, source_target_pairs={{0,8},{4,12},{8,16},{12,20},{16,24},{20,28},{24,0},{28,4},{1,9},{5... | collective-permute-start | bytes 294920 | tf_op jit(solution)/shard_map/ppermute | solution.py:252
  74.4 13.7 %collective-permute-start.15 = (bf16[2,2,16,768]{3,2,1,0:T(8,128)(2,1)S(1)}, bf16[2,2,16,768]{3,2,1,0:T(8,128)(2,1)S(1)}, u32[]{:S(2)}, u32[]{:S(2)}) collective-permute-start(bf16[2,2,16,768]{3,2,1,0:T(8,128)(2,1)S(1)} %get-tuple-element.55), channel_id=1, source_target_pairs={{0,24},{4,28},{8,0},{12,4},{16,8},{20,12},{24,16},{28,20},{1,25},{... | collective-permute-start | bytes 294920 | tf_op jit(solution)/shard_map/ppermute | solution.py:252
  78.5 12.2 %collective-permute-start.16 = (bf16[2,2,16,768]{3,2,1,0:T(8,128)(2,1)S(1)}, bf16[2,2,16,768]{3,2,1,0:T(8,128)(2,1)S(1)}, u32[]{:S(2)}, u32[]{:S(2)}) collective-permute-start(bf16[2,2,16,768]{3,2,1,0:T(8,128)(2,1)S(1)} %get-tuple-element.56), channel_id=1, source_target_pairs={{0,12},{4,16},{8,20},{12,24},{16,28},{20,0},{24,4},{28,8},{1,13},{... | collective-permute-start | bytes 294920 | tf_op jit(solution)/shard_map/ppermute | solution.py:252
  79.1 14.4 %collective-permute-start.17 = (bf16[2,2,16,768]{3,2,1,0:T(8,128)(2,1)S(1)}, bf16[2,2,16,768]{3,2,1,0:T(8,128)(2,1)S(1)}, u32[]{:S(2)}, u32[]{:S(2)}) collective-permute-start(bf16[2,2,16,768]{3,2,1,0:T(8,128)(2,1)S(1)} %get-tuple-element.57), channel_id=1, source_target_pairs={{0,20},{4,24},{8,28},{12,0},{16,4},{20,8},{24,12},{28,16},{1,21},{... | collective-permute-start | bytes 294920 | tf_op jit(solution)/shard_map/ppermute | solution.py:252
  83.6 10.1 %collective-permute-start.18 = (bf16[2,2,16,768]{3,2,1,0:T(8,128)(2,1)S(1)}, bf16[2,2,16,768]{3,2,1,0:T(8,128)(2,1)S(1)}, u32[]{:S(2)}, u32[]{:S(2)}) collective-permute-start(bf16[2,2,16,768]{3,2,1,0:T(8,128)(2,1)S(1)} %get-tuple-element.58), channel_id=1, source_target_pairs={{0,16},{4,20},{8,24},{12,28},{16,0},{20,4},{24,8},{28,12},{1,17},{... | collective-permute-start | bytes 294920 | tf_op jit(solution)/shard_map/ppermute | solution.py:252
  96.0 10.3 %all-to-all-start.2 = ((bf16[8,2,16,768]{3,2,1,0:T(8,128)(2,1)}), bf16[8,2,16,768]{3,2,1,0:T(8,128)(2,1)S(1)}, u32[]{:S(2)}, u32[]{:S(2)}) async-start(bf16[8,2,16,768]{3,2,1,0:T(8,128)(2,1)} %second_down.1), calls=%async_computation.2 | async-start | bytes 786432 | tf_op jit(solution)/shard_map/all_to_all | solution.py:267
  106.3 13.5 %all-to-all-start.1 = ((bf16[8,2,16,768]{3,2,1,0:T(8,128)(2,1)}), bf16[8,2,16,768]{3,2,1,0:T(8,128)(2,1)S(1)}, u32[]{:S(2)}, u32[]{:S(2)}) async-start(bf16[8,2,16,768]{3,2,1,0:T(8,128)(2,1)} %second_up.1), calls=%async_computation.1 | async-start | bytes 786432 | tf_op jit(solution)/shard_map/all_to_all | solution.py:267
  111.8 12.2 %collective-permute-start.22 = (bf16[8,16,768]{2,1,0:T(8,128)(2,1)S(1)}, bf16[8,16,768]{2,1,0:T(8,128)(2,1)S(1)}, u32[]{:S(2)}, u32[]{:S(2)}) collective-permute-start(bf16[8,16,768]{2,1,0:T(8,128)(2,1)S(1)} %get-tuple-element.64), channel_id=1, source_target_pairs={{0,24},{4,12},{8,0},{12,20},{16,8},{20,28},{24,16},{28,4},{1,25},{... | collective-permute-start | bytes 589832 | tf_op jit(solution)/shard_map/ppermute | solution.py:255
  116.5 12.3 %collective-permute-start.23 = (bf16[8,16,768]{2,1,0:T(8,128)(2,1)S(1)}, bf16[8,16,768]{2,1,0:T(8,128)(2,1)S(1)}, u32[]{:S(2)}, u32[]{:S(2)}) collective-permute-start(bf16[8,16,768]{2,1,0:T(8,128)(2,1)S(1)} %get-tuple-element.65), channel_id=1, source_target_pairs={{0,4},{4,8},{8,12},{12,16},{16,20},{20,24},{24,28},{28,0},{1,5},{5... | collective-permute-start | bytes 589832 | tf_op jit(solution)/shard_map/ppermute | solution.py:252
  116.7 12.2 %collective-permute-start.24 = (bf16[8,16,768]{2,1,0:T(8,128)(2,1)S(1)}, bf16[8,16,768]{2,1,0:T(8,128)(2,1)S(1)}, u32[]{:S(2)}, u32[]{:S(2)}) collective-permute-start(bf16[8,16,768]{2,1,0:T(8,128)(2,1)S(1)} %get-tuple-element.66), channel_id=1, source_target_pairs={{0,28},{4,0},{8,4},{12,8},{16,12},{20,16},{24,20},{28,24},{1,29},{... | collective-permute-start | bytes 589832 | tf_op jit(solution)/shard_map/ppermute | solution.py:252
  120.4 9.9 %collective-permute-start.19 = (bf16[8,16,768]{2,1,0:T(8,128)(2,1)S(1)}, bf16[8,16,768]{2,1,0:T(8,128)(2,1)S(1)}, u32[]{:S(2)}, u32[]{:S(2)}) collective-permute-start(bf16[8,16,768]{2,1,0:T(8,128)(2,1)S(1)} %get-tuple-element.60), channel_id=1, source_target_pairs={{0,24},{4,12},{8,0},{12,20},{16,8},{20,28},{24,16},{28,4},{1,25},{... | collective-permute-start | bytes 589832 | tf_op jit(solution)/shard_map/ppermute | solution.py:255
  123.9 12.3 %collective-permute-start.20 = (bf16[8,16,768]{2,1,0:T(8,128)(2,1)S(1)}, bf16[8,16,768]{2,1,0:T(8,128)(2,1)S(1)}, u32[]{:S(2)}, u32[]{:S(2)}) collective-permute-start(bf16[8,16,768]{2,1,0:T(8,128)(2,1)S(1)} %get-tuple-element.61), channel_id=1, source_target_pairs={{0,4},{4,8},{8,12},{12,16},{16,20},{20,24},{24,28},{28,0},{1,5},{5... | collective-permute-start | bytes 589832 | tf_op jit(solution)/shard_map/ppermute | solution.py:252
  124.0 12.2 %collective-permute-start.21 = (bf16[8,16,768]{2,1,0:T(8,128)(2,1)S(1)}, bf16[8,16,768]{2,1,0:T(8,128)(2,1)S(1)}, u32[]{:S(2)}, u32[]{:S(2)}) collective-permute-start(bf16[8,16,768]{2,1,0:T(8,128)(2,1)S(1)} %get-tuple-element.62), channel_id=1, source_target_pairs={{0,28},{4,0},{8,4},{12,8},{16,12},{20,16},{24,20},{28,24},{1,29},{... | collective-permute-start | bytes 589832 | tf_op jit(solution)/shard_map/ppermute | solution.py:252
  (9 other events, 93.4 us)
